TPU v7x, 128 devices: a whole 4x4x4 slice. The times are simulated.
128 devices in a mesh: group: 2 (over y_lo), replica: 64 (over y_hi, x, z, core).
Axes of the slice: x: 4, y: 4 (y_hi: 2, y_lo: 2; y = y_hi * 2 + y_lo), z: 4, core: 2. Of those that a mesh axis runs over, the one named last changes fastest.
Arguments:
- block_input: bfloat16 [16384, 1024], P(('group', 'replica')), may hold values from -6 to 6
- segment_ids: int32 [128, 128], P(('group', 'replica')), may hold values from 0 to 2, as said below
- ln1_gain: bfloat16 [1024], P('group'), may hold values from 0.5 to 1.5
- ln1_bias: bfloat16 [1024], P('group'), may hold values from -1.75 to 1.75
- w_qkv: bfloat16 [1024, 3072], P('group'), may hold values from -0.1875 to 0.1875
- b_query: bfloat16 [1024], P('group'), may hold values from -1.75 to 1.75
- b_value: bfloat16 [1024], P('group'), may hold values from -1.75 to 1.75
- w_out: bfloat16 [1024, 1024], P('group'), may hold values from -0.75 to 0.75
- b_out: bfloat16 [1024], P('group'), may hold values from -1.75 to 1.75
- ln2_gain: bfloat16 [1024], P('group'), may hold values from 0.5 to 1.5
- ln2_bias: bfloat16 [1024], P('group'), may hold values from -1.75 to 1.75
- w_fc: bfloat16 [1024, 4096], P('group'), may hold values from -0.1875 to 0.1875
- b_fc: bfloat16 [4096], P('group'), may hold values from -1.75 to 1.75
- w_proj: bfloat16 [4096, 1024], P('group'), may hold values from -0.09375 to 0.09375
- b_proj: bfloat16 [1024], P('group'), may hold values from -1.75 to 1.75
- cotangent: bfloat16 [16384, 1024], P(('group', 'replica')), may hold values from -6 to 6
Outputs:
- layer_output: bfloat16 [16384, 1024], P(('group', 'replica'))
- input_grad: float32 [16384, 1024], P(('group', 'replica'))
- ln1_gain_grad: float32 [1024], P('group')
- ln1_bias_grad: float32 [1024], P('group')
- w_qkv_grad: float32 [1024, 3072], P('group')
- b_query_grad: float32 [1024], P('group')
- b_value_grad: float32 [1024], P('group')
- w_out_grad: float32 [1024, 1024], P('group')
- b_out_grad: float32 [1024], P('group')
- ln2_gain_grad: float32 [1024], P('group')
- ln2_bias_grad: float32 [1024], P('group')
- w_fc_grad: float32 [1024, 4096], P('group')
- b_fc_grad: float32 [4096], P('group')
- w_proj_grad: float32 [4096, 1024], P('group')
- b_proj_grad: float32 [1024], P('group')
Inputs may be any that keep to these rules, and one draw needn't show every extreme that they name: Each row of segment_ids (one sequence) holds three documents numbered 0, 1, 2 in order, each of 25 tokens or more.
All inputs are finite; a program needn't handle non-finite values.
Results may differ from a plain program's by a relative error of at most 0.014.
Values may be sent and summed in bfloat16 or wider, within the bound.
No kernel may reach another device: no remote copies, remote signals or barrier semaphores. Data moves between devices by JAX's collectives and lax.ppermute only.
A program may use at most 256 MiB of HBM per device.

v0:
```python
import math

import jax
import jax.numpy as jnp
import numpy as np
from jax import lax
from jax.experimental import pallas as pl
from jax.experimental.pallas import tpu as pltpu
from jax.sharding import PartitionSpec as P

D = 1024
HEADS = 16
BATCH = 8
HEAD_DIM = 64
ROWS = 128
BOTH = 2 * ROWS
EXTRA = 16

norm_epsilon = 1e-05
masked_score = -1e30
gelu_factor = 0.7978845608028654
score_scale = 1.0 / math.sqrt(HEAD_DIM)

f32 = jnp.float32
bf16 = jnp.bfloat16
AXES = ("group", "replica")
MIB = 2**20


def flat(g, yh, x, z, c):
    return (((g * 2 + yh) * 4 + x) * 4 + z) * 2 + c


def at(y, x, z, c):
    return flat(y % 2, y // 2, x, z, c)


def everywhere():
    return [(g, yh, x, z, c) for g in range(2) for yh in range(2) for x in range(4) for z in range(4) for c in range(2)]


def exchange(move):
    return [(flat(g, yh, x, z, c), move(2 * yh + g, x, z, c)) for g, yh, x, z, c in everywhere()]


FIRST = {
    "g": exchange(lambda y, x, z, c: at(y ^ (1, 3)[c], x, z, c)),
    "x": exchange(lambda y, x, z, c: at(y, x ^ (1, 3)[c], z, c)),
    "z": exchange(lambda y, x, z, c: at(y, x, z ^ (1, 3)[c], c)),
    "xz": exchange(lambda y, x, z, c: at(y, x ^ (1, 3)[c], z ^ (1, 3)[c], c)),
}
SECOND = {
    "x": exchange(lambda y, x, z, c: at(y, x ^ (3, 1)[c], z, c)),
    "z": exchange(lambda y, x, z, c: at(y, x, z ^ (3, 1)[c], c)),
    "xz": exchange(lambda y, x, z, c: at(y, x ^ (3, 1)[c], z ^ (3, 1)[c], c)),
}
FAR = exchange(lambda y, x, z, c: at(y ^ 2, x, z, c))
CORE = exchange(lambda y, x, z, c: at(y, x, z, c ^ 1))


def swap(array, pairs):
    return lax.ppermute(array, AXES, pairs)


def after(value, *others):
    return lax.optimization_barrier((value, others))[0]


G, C, UX, UZ, VX, VZ = range(6)
PIECE = 6
QUARTER = 9
NUMBERS = 16


def numbers():
    rows = []
    for g, yh, x, z, c in everywhere():
        xs = ((x % 2) ^ (x // 2), x // 2)
        zs = ((z % 2) ^ (z // 2), z // 2)
        ux, vx, uz, vz = xs[c], xs[1 - c], zs[c], zs[1 - c]
        base = (1 - g) * 512
        row = [g, c, ux, uz, vx, vz, g * 512, base + c * 256, base + (1 - c) * 256]
        row += [base + ((ux ^ rx) * 2 + (uz ^ rz)) * 128 for rx in range(2) for rz in range(2)]
        rows.append(row + [0] * (NUMBERS - len(row)))
    return np.array(rows, np.int32)


def cost(us):
    return pl.CostEstimate(flops=0, bytes_accessed=int(us * 3.69e6), transcendentals=0)


def shape(dims, dtype):
    return jax.ShapeDtypeStruct(dims, dtype)


def dot(left, right):
    return jnp.dot(left, right, preferred_element_type=f32)


def rows_dot(left, right):
    return lax.dot_general(left, right, (((0,), (0,)), ((), ())), preferred_element_type=f32)


def dot_rows(left, right):
    return lax.dot_general(left, right, (((1,), (1,)), ((), ())), preferred_element_type=f32)


def span(start, size):
    return pl.ds(pl.multiple_of(start, size), size)


def norm_parts(values):
    center = jnp.mean(values, axis=-1, keepdims=True)
    centered = values - center
    variance = jnp.mean(centered * centered, axis=-1, keepdims=True)
    scale = lax.rsqrt(variance + norm_epsilon)
    return centered * scale, scale


def norm_back(normal, scale, grad):
    return scale * (
        grad
        - jnp.mean(grad, axis=-1, keepdims=True)
        - normal * jnp.mean(grad * normal, axis=-1, keepdims=True)
    )


def over(values):
    return jnp.sum(values, axis=0, keepdims=True)


MADE = []


def stepped(body, steps, table, operands, in_specs, outputs, out_specs, estimate, scratch=(), limit=32, near=False):
    operands = [
        pltpu.with_memory_space_constraint(array, pltpu.HBM)
        if not near and array.size >= 32768 and not any(array is made for made in MADE)
        else array
        for array in operands
    ]
    results = pl.pallas_call(
        body,
        grid_spec=pltpu.PrefetchScalarGridSpec(
            num_scalar_prefetch=1,
            grid=(steps,),
            in_specs=in_specs,
            out_specs=out_specs,
            scratch_shapes=list(scratch),
        ),
        out_shape=outputs,
        compiler_params=pltpu.CompilerParams(vmem_limit_bytes=limit * MIB),
        cost_estimate=estimate,
    )(table, *operands)
    MADE.extend(jax.tree.leaves(results))
    return results


def block(dims, place):
    return pl.BlockSpec(dims, place)


def fixed(dims, row=0, column=0):
    place = (row, column) if len(dims) == 2 else (0,) * len(dims)
    return pl.BlockSpec(dims, lambda j, t: place)


FIRST_ROWS = 256 + ROWS + EXTRA


def pack(table, inputs, w_out, w_fc, vectors):
    def body(t, in_ref, out_ref, low_ref, high_ref, *refs):
        first, fc_part = refs[9:]
        first[:256, :] = out_ref[...]
        first[256:384, :] = in_ref[...]
        first[384:, :] = jnp.zeros((EXTRA, D), bf16)
        for k in range(8):
            first[384 + k // 2 : 385 + k // 2, 512 * (k % 2) : 512 * (k % 2) + 512] = refs[k][...].reshape(1, 512)
        for k in range(2):
            first[388 + k : 389 + k, :] = refs[8][pl.ds(1024 * k, 1024)].reshape(1, 1024)
        fc_part[:, :1024] = low_ref[...]
        fc_part[:, 1024:] = high_ref[...]

    outputs = [shape((FIRST_ROWS, D), bf16), shape((128, 2048), bf16)]
    return stepped(
        body,
        1,
        table,
        (inputs, w_out, w_fc, w_fc, *vectors),
        [
            fixed((ROWS, D)),
            block((256, D), lambda j, t: (t[C], 0)),
            block((128, 1024), lambda j, t: (t[UX] * 2 + t[UZ], t[C])),
            block((128, 1024), lambda j, t: (t[UX] * 2 + t[UZ], 2 + t[C])),
        ]
        + [pl.BlockSpec(v.shape, lambda j, t: (0,)) for v in vectors],
        outputs,
        [fixed(o.shape) for o in outputs],
        cost(3.6),
        limit=60,
    )


def spread(table, own, other):
    def body(t, own_ref, other_ref, full_ref, bias_ref):
        first = t[G] == 0
        mine = own_ref[...].astype(f32)[:8]
        theirs = other_ref[...].astype(f32)[:8]
        low = jnp.where(first, mine, theirs)
        high = jnp.where(first, theirs, mine)
        for k in range(8):
            half = slice(512 * (k % 2), 512 * (k % 2) + 512)
            full_ref[k : k + 1, :512] = low[k // 2 : k // 2 + 1, half]
            full_ref[k : k + 1, 512:] = high[k // 2 : k // 2 + 1, half]
        second = t[C] == 1
        bias_ref[:, :1024] = jnp.where(second, low[5:6], low[4:5])
        bias_ref[:, 1024:] = jnp.where(second, high[5:6], high[4:5])

    tail = fixed((EXTRA, D), 384 // EXTRA)
    return stepped(
        body,
        1,
        table,
        (own, other),
        [tail, tail],
        [shape((8, D), f32), shape((1, 2048), f32)],
        [fixed((8, D)), fixed((1, 2048))],
        cost(1),
    )


def project(table, own, other, gain, shift, w_qkv):
    width = 512

    def body(t, own_ref, other_ref, gain_ref, shift_ref, w_ref, mine_ref, theirs_ref, normed_ref):
        @pl.when(pl.program_id(0) == 0)
        def _():
            half = span(t[PIECE], 512)
            scale = gain_ref[...].astype(f32).reshape(1, 512)
            offset = shift_ref[...].astype(f32).reshape(1, 512)
            for k, ref in enumerate((own_ref, other_ref)):
                values = ref[...].astype(f32)
                center = jnp.mean(values, axis=-1, keepdims=True)
                centered = values - center
                variance = jnp.mean(centered * centered, axis=-1, keepdims=True)
                part = (ref[:, half].astype(f32) - center) * lax.rsqrt(variance + norm_epsilon)
                normed_ref[k * ROWS : (k + 1) * ROWS, :] = (part * scale + offset).astype(bf16)

        total = dot(normed_ref[...], w_ref[...])
        mine_ref[...] = total[:ROWS]
        theirs_ref[...] = total[ROWS:].astype(bf16)

    step = lambda j, t: (0, j)
    vector = pl.BlockSpec((512,), lambda j, t: (0,))
    return stepped(
        body,
        6,
        table,
        (own, other, gain, shift, w_qkv),
        [fixed((ROWS, D), 2), fixed((ROWS, D), 2), vector, vector, block((512, width), step)],
        [shape((ROWS, 3 * D), f32), shape((ROWS, 3 * D), bf16)],
        [block((ROWS, width), step), block((ROWS, width), step)],
        cost(8),
        [pltpu.VMEM((BOTH, 512), bf16)],
    )


def admitted(segments_ref):
    across = jnp.broadcast_to(segments_ref[...], (ROWS, ROWS))
    down = across.T
    row = lax.broadcasted_iota(jnp.int32, (ROWS, ROWS), 0)
    column = lax.broadcasted_iota(jnp.int32, (ROWS, ROWS), 1)
    return (row >= column) & (across == down)


def cut_heads(ref, first, heads):
    return [ref[:, first + head * HEAD_DIM : first + (head + 1) * HEAD_DIM] for head in heads]


def head_probs(projected_ref, heads, allowed):
    queries, keys, values = (cut_heads(projected_ref, k * D, heads) for k in range(3))
    scores = [jnp.where(allowed, dot_rows(q, k) * score_scale, masked_score) for q, k in zip(queries, keys)]
    weights = [jnp.exp(x - jnp.max(x, axis=-1, keepdims=True)) for x in scores]
    return queries, keys, values, [x / jnp.sum(x, axis=-1, keepdims=True) for x in weights]


def mix(table, mine, theirs, full, segments):
    def body(t, mine_ref, theirs_ref, full_ref, seg_ref, p_ref, mixture_ref):
        for k, row in ((0, 2), (1, None), (2, 3)):
            columns = slice(k * D, (k + 1) * D)
            total = mine_ref[:, columns] + theirs_ref[:, columns].astype(f32)
            if row is not None:
                total += full_ref[row : row + 1, :]
            p_ref[:, columns] = total.astype(bf16)
        allowed = admitted(seg_ref)
        _, _, values, probs = head_probs(p_ref, range(HEADS), allowed)
        outputs = [dot(p.astype(bf16), v).astype(bf16) for p, v in zip(probs, values)]
        for head, output in enumerate(outputs):
            mixture_ref[:, head * HEAD_DIM : (head + 1) * HEAD_DIM] = output

    return stepped(
        body,
        1,
        table,
        (mine, theirs, full, segments),
        [fixed((ROWS, 3 * D)), fixed((ROWS, 3 * D)), fixed((8, D)), fixed((1, ROWS))],
        [shape((ROWS, 3 * D), bf16), shape((ROWS, D), bf16)],
        [fixed((ROWS, 3 * D)), fixed((ROWS, D))],
        cost(8.1),
    )


def settle(table, mixture, inputs, full, w_out, near, far):
    def body(t, mixture_ref, in_ref, full_ref, own, a, b, side_ref, residual_ref):
        total = dot(mixture_ref[:, span(t[PIECE], 512)], own[...])
        for k, ref in enumerate((a, b)):
            total += dot(mixture_ref[:, span(t[PIECE + 1 + k], 256)], ref[...])
        residual = in_ref[...].astype(f32) + (total + full_ref[4:5, :])
        residual_ref[...] = residual
        normal, _ = norm_parts(residual)
        side_ref[:, :D] = (normal * full_ref[5:6, :] + full_ref[6:7, :]).astype(bf16)
        side_ref[:, D:] = mixture_ref[...]

    return stepped(
        body,
        1,
        table,
        (mixture, inputs, full, w_out, near, far),
        [fixed((ROWS, D)), fixed((ROWS, D)), fixed((8, D)), fixed((512, D)), fixed((256, D)), fixed((256, D))],
        [shape((ROWS, 2 * D), bf16), shape((ROWS, D), f32)],
        [fixed((ROWS, 2 * D)), fixed((ROWS, D))],
        cost(3),
    )


def feed_forward(table, side, early, w_fc, quarters, bias, w_proj, others, full):
    def units(j, t):
        return jnp.where(j % 4 < 2, t[G], 1 - t[G]) * 2 + j % 2

    def body(t, *refs):
        side_ref, early_refs, own_fc, pieces_fc = refs[0], refs[1:5], refs[5], refs[6:10]
        bias_ref, low_ref, high_ref, own_proj, first_proj, second_proj, full_ref = refs[10:17]
        hidden_ref, grad_ref, sums_ref, back_mine, back_theirs, out_mine, out_theirs, normed_ref, slope_ref = refs[17:]
        j = pl.program_id(0)
        k = j % 4
        columns = span(units(j, t) * 512, 512)

        @pl.when(j < 4)
        def _():
            here = span(k * 512, 512)
            values = dot(side_ref[:, span(t[PIECE], 512)], own_fc[...])
            for i, ref in enumerate(pieces_fc):
                values += dot(side_ref[:, span(t[QUARTER + i], 128)], ref[:, here])
            values += bias_ref[:, here]
            square = values * values
            inner = jnp.tanh(gelu_factor * values * (1.0 + 0.044715 * square))
            outer = 0.5 * (1.0 + inner)
            hidden_ref[:, here] = (values * outer).astype(bf16)
            slope_ref[:, here] = outer + values * outer * (1.0 - inner) * gelu_factor * (1.0 + 3.0 * 0.044715 * square)

        def with_proj(use):
            for ref, wanted in ((own_proj, k < 2), (first_proj, k == 2), (second_proj, k == 3)):

                @pl.when(wanted)
                def _():
                    use(ref[...])

        @pl.when((j >= 4) & (j < 8))
        def _():
            def use(weights):
                grad = (dot_rows(early_refs[0][:, :D], weights) * slope_ref[:, columns]).astype(bf16)
                grad_ref[:, columns] = grad
                sums_ref[:, columns] = over(grad.astype(f32))

            with_proj(use)

        @pl.when((j >= 8) & (j < 12))
        def _():
            def use(low, high, first, size):
                total = dot_rows(grad_ref[:, :1024], low) + dot_rows(grad_ref[:, 1024:], high)
                back_mine[:, span(first, size)] = total[:ROWS]
                back_theirs[:, span(first, size)] = total[ROWS:]

            @pl.when(k < 2)
            def _():
                use(low_ref[...], high_ref[...], t[G] * 512 + k * 256, 256)

            for step in (2, 3):

                @pl.when(k == step)
                def _():
                    for i in (2 * step - 4, 2 * step - 3):
                        use(pieces_fc[i][:, :1024], pieces_fc[i][:, 1024:], t[QUARTER + i], 128)

        @pl.when((j >= 12) & (j < 16))
        def _():
            def use(weights):
                total = dot(hidden_ref[:, columns], weights)

                @pl.when(k == 0)
                def _():
                    out_mine[...] = total[:ROWS]
                    out_theirs[...] = total[ROWS:]

                @pl.when(k > 0)
                def _():
                    out_mine[...] += total[:ROWS]
                    out_theirs[...] += total[ROWS:]

            with_proj(use)

        for i, ref in enumerate(early_refs):

            @pl.when(j == 16 + i)
            def _():
                normal, _ = norm_parts(ref[:, D:].astype(f32))
                normed_ref[...] = (normal * full_ref[0:1, :] + full_ref[1:2, :]).astype(bf16)

    def back_rows(j):
        return jnp.clip(j - 8, 0, 1)

    def proj_rows(j, t):
        return (t[C] * 2 + jnp.where((j == 4) | (j < 4) | (j == 12), 0, 1), 0)

    square = fixed((ROWS, D))
    return stepped(
        body,
        20,
        table,
        (side, *early, w_fc, *quarters, bias, w_fc, w_fc, w_proj, *others, full),
        [fixed((BOTH, D))]
        + [fixed((BOTH, 2 * D))] * 4
        + [block((512, 512), lambda j, t: (0, jnp.minimum(j, 3) // 2 * 4 + t[C] * 2 + jnp.minimum(j, 3) % 2))]
        + [fixed((128, 2048), row) for row in (0, 0, 0, 1)]
        + [fixed((1, 2048))]
        + [block((256, 1024), lambda j, t: (back_rows(j), t[C])), block((256, 1024), lambda j, t: (back_rows(j), 2 + t[C]))]
        + [block((512, D), proj_rows), fixed((512, D)), fixed((512, D)), fixed((8, D))],
        [shape((BOTH, 2048), bf16), shape((BOTH, 2048), bf16), shape((1, 2048), f32)]
        + [shape((ROWS, D), f32)] * 4
        + [shape((4 * BOTH, D), bf16)],
        [fixed((BOTH, 2048)), fixed((BOTH, 2048)), fixed((1, 2048)), square, square, square, square]
        + [block((BOTH, D), lambda j, t: (jnp.clip(j - 16, 0, 3), 0))],
        cost(23),
        [pltpu.VMEM((BOTH, 2048), f32)],
        limit=48,
    )


def attend_back(table, mine, theirs, residual, cotangent, full, projected, segments, w_out, near, far):
    def body(
        t, mine_ref, theirs_ref, res_ref, cot_ref, full_ref, p_ref, seg_ref, own, a, b,
        grad_ref, dealt_ref, sums_ref, mix_ref,
    ):
        normal, scale = norm_parts(res_ref[...])
        grad_normed = mine_ref[...] + theirs_ref[...]
        grad_output = cot_ref[...].astype(f32)
        grad = grad_output + norm_back(normal, scale, grad_normed * full_ref[5:6, :])
        grad_ref[...] = grad
        low = grad.astype(bf16)
        for k in range(8):
            dealt_ref[k // 4, :, 512 * (k % 4) + 384 : 512 * (k % 4) + 512] = low[:, 128 * k : 128 * (k + 1)]
        sums_ref[0:1, :] = over(grad)
        sums_ref[1:2, :] = over(grad_normed * normal)
        sums_ref[2:3, :] = over(grad_normed)
        sums_ref[3:4, :] = over(grad_output)
        sums_ref[4:, :] = jnp.zeros((4, D), f32)
        mix_ref[:, span(t[PIECE], 512)] = dot_rows(low, own[...]).astype(bf16)
        for k, ref in enumerate((a, b)):
            mix_ref[:, span(t[PIECE + 1 + k], 256)] = dot_rows(low, ref[...]).astype(bf16)
        allowed = admitted(seg_ref)

        def store(number, values):
            column = 512 * (number % 24 // 6) + HEAD_DIM * (number % 6)
            dealt_ref[number // 24, :, column : column + HEAD_DIM] = values.astype(bf16)

        for first in range(0, HEADS, BATCH):
            heads = range(first, first + BATCH)
            queries, keys, values, probs = head_probs(p_ref, heads, allowed)
            grad_mix = cut_heads(mix_ref, 0, heads)
            grad_probs = [dot_rows(g, v) for g, v in zip(grad_mix, values)]
            centres = [jnp.sum(p * g, axis=-1, keepdims=True) for p, g in zip(probs, grad_probs)]
            grad_scores = [(p * (g - x)).astype(bf16) for p, g, x in zip(probs, grad_probs, centres)]
            found = (
                [dot(g, k) * score_scale for g, k in zip(grad_scores, keys)],
                [rows_dot(g, q) * score_scale for g, q in zip(grad_scores, queries)],
                [rows_dot(p.astype(bf16), g) for p, g in zip(probs, grad_mix)],
            )
            for kind, results in enumerate(found):
                for head, result in zip(heads, results):
                    store(kind * HEADS + head, result)

    square = fixed((ROWS, D))
    return stepped(
        body,
        1,
        table,
        (mine, theirs, residual, cotangent, full, projected, segments, w_out, near, far),
        [square] * 4 + [fixed((8, D)), fixed((ROWS, 3 * D)), fixed((1, ROWS))]
        + [fixed((512, D)), fixed((256, D)), fixed((256, D))],
        [shape((ROWS, D), f32), shape((2, ROWS, 2048), bf16), shape((8, D), f32)],
        [square, fixed((2, ROWS, 2048)), fixed((8, D))],
        cost(11.5),
        [pltpu.VMEM((ROWS, D), bf16)],
    )


def input_back(table, dealt, w_qkv, near, far, inputs, grad_residual, full, sums, fc_sums):
    width = 384

    def body(t, grad_ref, own, a, b, in_ref, res_ref, full_ref, early_ref, fc_ref, out_ref, sums_ref, total_ref, bias_ref):
        j = pl.program_id(0)
        grad = grad_ref[0, :, :width]

        @pl.when(j == 0)
        def _():
            total_ref[...] = jnp.zeros((ROWS, D), f32)

        offset = 0
        for ref in (own, a, b):
            size = ref.shape[0]
            total_ref[:, offset : offset + size] += dot_rows(grad, ref[...])
            offset += size
        bias_ref[:, span(j * width, width)] = over(grad.astype(f32))

        @pl.when(j == 7)
        def _():
            offset = 0
            for k, size in enumerate((512, 256, 256)):
                out_ref[:, span(t[PIECE + k], size)] = total_ref[:, offset : offset + size]
                offset += size
            grad_normed = out_ref[...]
            normal, scale = norm_parts(in_ref[...].astype(f32))
            gain_sums = over(grad_normed * normal)
            shift_sums = over(grad_normed)
            out_ref[...] = res_ref[...] + norm_back(normal, scale, grad_normed * full_ref[0:1, :])
            row = lax.broadcasted_iota(jnp.int32, (4, 512), 0)
            for g in range(2):
                half = slice(512 * g, 512 * (g + 1))
                sums_ref[16 * g : 16 * g + 1, :] = gain_sums[:, half]
                sums_ref[16 * g + 1 : 16 * g + 2, :] = shift_sums[:, half]
                sums_ref[16 * g + 2 : 16 * g + 3, :] = bias_ref[:, 512 * g : 512 * (g + 1)]
                sums_ref[16 * g + 3 : 16 * g + 4, :] = bias_ref[:, 2048 + 512 * g : 2048 + 512 * (g + 1)]
                sums_ref[16 * g + 4 : 16 * g + 8, :] = early_ref[0:4, half]
                units = [fc_ref[:, 1024 * g + 512 * (k % 2) : 1024 * g + 512 * (k % 2) + 512] for k in range(4)]
                sums_ref[16 * g + 8 : 16 * g + 12, :] = jnp.where(row // 2 == t[C], jnp.concatenate(units, 0), 0.0)
                sums_ref[16 * g + 12 : 16 * g + 16, :] = jnp.zeros((4, 512), f32)

    step = lambda j, t: (0, j)
    return stepped(
        body,
        8,
        table,
        (dealt, w_qkv, near, far, inputs, grad_residual, full, sums, fc_sums),
        [pl.BlockSpec((1, ROWS, 512), lambda j, t: (j // 4, 0, j % 4)), block((512, width), step)]
        + [block((256, width), step)] * 2
        + [fixed((ROWS, D)), fixed((ROWS, D)), fixed((8, D)), fixed((8, D)), fixed((1, 2048))],
        [shape((ROWS, D), f32), shape((2 * EXTRA, 512), f32)],
        [fixed((ROWS, D)), fixed((2 * EXTRA, 512))],
        cost(9.2),
        [pltpu.VMEM((ROWS, D), f32), pltpu.VMEM((1, 3 * D), f32)],
    )


def piece_specs(pieces, width, number):
    specs, operands = [], []
    for array, row, column in pieces:
        specs.append(
            pl.BlockSpec(
                (BOTH, width),
                lambda j, t, row=row, column=column: (row(t) if callable(row) else row, column + number(j, t)),
            )
        )
        operands.append(array)
    return specs, operands


def sum_dots(lefts, rights, columns=slice(None)):
    total = rows_dot(lefts[0][...], rights[0][:, columns])
    for left, right in zip(lefts[1:], rights[1:]):
        total += rows_dot(left[...], right[:, columns])
    return total


def deal_feed(table, hidden, grad_pre):
    def body(t, hidden_ref, grad_ref, *outs):
        for j, out in enumerate(outs):
            away = 3 - j
            bx, bz = (away // 2) ^ t[UX], (away % 2) ^ t[UZ]
            for g in range(2):
                out[:, 256 * g : 256 * (g + 1)] = hidden_ref[:, span(g * 1024 + (bx * 2 + bz) * 256, 256)]
            out[:, 512:] = grad_ref[:, span((bx * 2 + bz) * 512, 512)]

    return stepped(
        body, 1, table, (hidden, grad_pre), [fixed((BOTH, 2048))] * 2, [shape((BOTH, D), bf16)] * 4,
        [fixed((BOTH, D))] * 4, cost(0.8), near=True,
    )


def deal_attention(table, mine, theirs):
    def body(t, mine_ref, theirs_ref, *outs):
        for j, out in enumerate(outs):
            away = 3 - j
            columns = span((((away // 2) ^ t[UX]) * 2 + ((away % 2) ^ t[UZ])) * 512, 512)
            out[:ROWS, :] = mine_ref[0, :, columns]
            out[ROWS:, :] = theirs_ref[:, columns]

    return stepped(
        body, 1, table, (mine, theirs),
        [pl.BlockSpec((1, ROWS, 2048), lambda j, t: (t[C], 0, 0)), fixed((ROWS, 2048))],
        [shape((BOTH, 512), bf16)] * 4, [fixed((BOTH, 512))] * 4, cost(0.7), near=True,
    )


def quarter(j, t):
    away = 3 - j
    return ((away // 2) ^ t[VX]) * 2 + ((away % 2) ^ t[VZ])


def half_rows(j, t):
    return jnp.where(j == 0, 1 - t[VX], t[VX])


def feed_specs(normeds, grads, hiddens, cotangents, rows, width, features, units, columns):
    specs, operands = [], []
    for pieces, size, number in (
        (normeds, rows, features),
        (grads, 512, lambda j, t: 1),
        (hiddens, 256, units),
        (cotangents, width, columns),
    ):
        more, arrays = piece_specs(pieces, size, number)
        specs += more
        operands += arrays
    return specs, operands


def feed_sent(table, normeds, grads, hiddens, cotangents):
    specs, operands = feed_specs(
        normeds, grads, hiddens, cotangents, 256, 512,
        lambda j, t: (1 - t[G]) * 2 + j, lambda j, t: 1 - t[G], lambda j, t: j,
    )

    def body(t, *refs):
        out = refs[-1]
        out[:, :512] = sum_dots(refs[:4], refs[4:8]).astype(bf16)
        units = sum_dots(refs[8:12], refs[12:16]).astype(bf16)
        for q in range(2):
            rows, columns = slice(128 * q, 128 * (q + 1)), slice(256 * q, 256 * (q + 1))
            out[rows, 512:768] = units[:128, columns]
            out[rows, 768:] = units[128:, columns]

    return stepped(
        body, 2, table, operands, specs, shape((512, D), bf16), block((256, D), lambda j, t: (j, 0)), cost(4.3),
    )


def feed_total(table, normeds, grads, hiddens, cotangents, received):
    specs, operands = feed_specs(
        normeds, grads, hiddens, cotangents, 128, 256,
        lambda j, t: t[G] * 4 + quarter(j, t), lambda j, t: t[G], quarter,
    )

    def body(t, *refs):
        received_ref = refs[16]
        outs = refs[17:]
        j = pl.program_id(0)
        got = received_ref[...].astype(f32)
        left = sum_dots(refs[:4], refs[4:8]) + got[:, :512]
        right = sum_dots(refs[8:12], refs[12:16])
        top = right[:128] + got[:, 512:768]
        low = right[128:] + got[:, 768:]
        for k, out in enumerate(outs):

            @pl.when(j == k)
            def _():
                out[:, :512] = left.astype(out.dtype)
                out[:, 512:768] = top.astype(out.dtype)
                out[:, 768:] = low.astype(out.dtype)

    return stepped(
        body,
        4,
        table,
        operands + [received],
        specs + [block((128, D), lambda j, t: (quarter(j, t), 0))],
        [shape((128, D), bf16)] * 3 + [shape((128, D), f32)],
        [fixed((128, D))] * 4,
        cost(5),
    )


def attention_sent(table, normeds, mixtures, grads, sums):
    specs, operands = [], []
    for pieces in (normeds, mixtures):
        more, arrays = piece_specs(pieces, 512, lambda j, t: 1 - t[G])
        specs += more
        operands += arrays
    more, arrays = piece_specs(grads, 512, lambda j, t: 0)

    def body(t, *refs):
        sums_ref, out_ref = refs[12:]
        out_ref[:512, :384] = sum_dots(refs[:4], refs[8:12], slice(0, 384)).astype(bf16)
        out_ref[:512, 384:] = sum_dots(refs[4:8], refs[8:12], slice(384, 512)).astype(bf16)
        out_ref[512:, :] = sums_ref[...].astype(bf16)

    return stepped(
        body,
        1,
        table,
        operands + arrays + [sums],
        specs + more + [block((EXTRA, 512), lambda j, t: (1 - t[G], 0))],
        shape((512 + EXTRA, 512), bf16),
        fixed((512 + EXTRA, 512)),
        cost(3.3),
    )


def attention_total(table, normeds, mixtures, grads, received, sums):
    specs, operands = [], []
    for pieces in (normeds, mixtures):
        more, arrays = piece_specs(pieces, 256, lambda j, t: t[G] * 2 + half_rows(j, t))
        specs += more
        operands += arrays
    more, arrays = piece_specs(grads, 512, lambda j, t: 0)

    def body(t, *refs):
        received_ref, tail_ref, sums_ref, sent_ref, kept_ref, total_ref = refs[12:]
        j = pl.program_id(0)
        got = received_ref[...].astype(f32)
        left = sum_dots(refs[:4], refs[8:12], slice(0, 384)) + got[:, :384]
        right = sum_dots(refs[4:8], refs[8:12], slice(384, 512)) + got[:, 384:]

        @pl.when(j == 0)
        def _():
            sent_ref[:256, :384] = left.astype(bf16)
            sent_ref[:256, 384:] = right.astype(bf16)
            total = sums_ref[...] + tail_ref[...].astype(f32)
            total_ref[...] = total
            sent_ref[256:, :] = total.astype(bf16)

        @pl.when(j == 1)
        def _():
            kept_ref[:, :384] = left
            kept_ref[:, 384:] = right

    return stepped(
        body,
        2,
        table,
        operands + arrays + [received, received, sums],
        specs
        + more
        + [
            block((256, 512), lambda j, t: (half_rows(j, t), 0)),
            fixed((EXTRA, 512), 512 // EXTRA),
            block((EXTRA, 512), lambda j, t: (t[G], 0)),
        ],
        [shape((256 + EXTRA, 512), bf16), shape((256, 512), f32), shape((EXTRA, 512), f32)],
        [fixed((256 + EXTRA, 512)), fixed((256, 512)), fixed((EXTRA, 512))],
        cost(3.9),
    )


def add_up(table, kept, received):
    def body(t, kept_ref, *refs):
        total = kept_ref[...].astype(f32)
        for ref in refs[:-1]:
            total += ref[...].astype(f32)
        refs[-1][...] = total.astype(bf16)

    operands = [kept, *received]
    return stepped(
        body, 1, table, operands, [fixed(a.shape) for a in operands], shape(kept.shape, bf16), fixed(kept.shape),
        cost(0.7),
        near=True,
    )


def place_quarters(table, mine, others):
    width = mine.shape[1]
    extra = mine.shape[0] - 128

    def body(t, *refs):
        out = refs[-1]
        for j, ref in enumerate(refs[:-1]):
            out[span(quarter(j, t) * 128, 128), :] = ref[:128, :]
        if extra:
            out[512:, :] = refs[3][128:, :]

    operands = [*others, mine]
    return stepped(
        body, 1, table, operands, [fixed(a.shape) for a in operands], shape((512 + extra, width), bf16),
        fixed((512 + extra, width)), cost(0.7),
        near=True,
    )


def add_split(table, kept, received, sums):
    rows, width = kept.shape
    half, extra = rows // 2, received.shape[0] - rows

    def body(t, kept_ref, received_ref, *refs):
        sent_ref, left_ref = refs[-3:-1] if extra else refs
        for bit, out in ((1 - t[VZ], sent_ref), (t[VZ], left_ref)):
            lines = span(bit * half, half)
            total = kept_ref[lines, :] + received_ref[lines, :].astype(f32)
            out[:half, :] = total.astype(out.dtype)
        if extra:
            total = refs[0][...] + received_ref[rows:, :].astype(f32)
            refs[-1][...] = total
            sent_ref[half:, :] = total.astype(bf16)

    outputs = [shape((half + extra, width), bf16), shape((half, width), f32)]
    if extra:
        outputs.append(shape((extra, width), f32))
    operands = [kept, received] + ([sums] if extra else [])
    return stepped(
        body, 1, table, operands, [fixed(a.shape) for a in operands], outputs, [fixed(o.shape) for o in outputs],
        cost(0.7),
        near=True,
    )


def add_low(table, kept, received, sums):
    rows, width = kept.shape
    extra = received.shape[0] - rows

    def body(t, kept_ref, received_ref, *refs):
        out = refs[-1]
        out[:rows, :] = (kept_ref[...] + received_ref[:rows, :].astype(f32)).astype(bf16)
        if extra:
            out[rows:, :] = (refs[0][...] + received_ref[rows:, :].astype(f32)).astype(bf16)

    operands = [kept, received] + ([sums] if extra else [])
    return stepped(
        body, 1, table, operands, [fixed(a.shape) for a in operands], shape(received.shape, bf16),
        fixed(received.shape), cost(0.6),
        near=True,
    )


def add_far(table, low, received, extra):
    rows, width = low.shape[0] - extra, low.shape[1]

    def body(t, low_ref, received_ref, *outs):
        total = low_ref[...].astype(f32) + received_ref[...].astype(f32)
        outs[0][...] = total[:rows].astype(bf16)
        if extra:
            outs[1][...] = total[rows:].astype(bf16)

    outputs = [shape((rows, width), bf16)] + ([shape((extra, width), bf16)] if extra else [])
    return stepped(
        body, 1, table, (low, received), [fixed(low.shape)] * 2, outputs, [fixed(o.shape) for o in outputs],
        cost(0.6),
        near=True,
    )


def place(table, bit, mine, other, sums=None):
    rows, width = mine.shape
    extra = 0 if sums is None else EXTRA

    def body(t, mine_ref, other_ref, *refs):
        out = refs[-1]
        out[span(t[bit] * rows, rows), :] = mine_ref[...]
        out[span((1 - t[bit]) * rows, rows), :] = other_ref[...]
        if extra:
            out[2 * rows :, :] = refs[0][...]

    operands = [mine, other] + ([sums] if extra else [])
    return stepped(
        body, 1, table, operands, [fixed(a.shape) for a in operands], shape((2 * rows + extra, width), bf16),
        fixed((2 * rows + extra, width)), cost(0.6),
        near=True,
    )


def targets(t):
    found = []
    for k in range(8):
        core = t[C] if k < 4 else 1 - t[C]
        ux, uz = (t[UX], t[UZ]) if k < 4 else (t[VX], t[VZ])
        found.append((core, ((k // 2 % 2) ^ ux) * 2 + ((k % 2) ^ uz)))
    return found


def unpack_feed(table, arrays):
    def body(t, *refs):
        fc_ref, proj_ref = refs[8:]
        rows = span(pl.program_id(0) * 128, 128)
        for ref, (core, number) in zip(refs, targets(t)):
            fc_ref[:, span((number // 2) * 2048 + core * 1024 + (number % 2) * 512, 512)] = ref[rows, :512].astype(f32)
            proj_ref[core * 4 + number, :128, :] = ref[rows, 512:768].astype(f32)
            proj_ref[core * 4 + number, 128:, :] = ref[rows, 768:].astype(f32)

    fc_grad, proj_grad = stepped(
        body,
        4,
        table,
        arrays,
        [pl.BlockSpec(memory_space=pltpu.VMEM)] * 8,
        [shape((512, 4096), f32), shape((8, 256, D), f32)],
        [block((128, 4096), lambda j, t: (j, 0)), pl.BlockSpec((8, 256, 256), lambda j, t: (0, 0, j))],
        cost(7),
        near=True,
    )
    return fc_grad, proj_grad.reshape(2048, D)


def unpack_attention(table, arrays):
    def body(t, *refs):
        arrays, qkv_ref, out_ref, vectors = refs[:8], refs[8], refs[9], refs[10:]
        rows = span(pl.program_id(0) * 128, 128)
        for ref, (core, number) in zip(arrays, targets(t)):
            qkv_ref[:, span((core * 4 + number) * 384, 384)] = ref[rows, :384].astype(f32)
            out_ref[:, span((core * 4 + number) * 128, 128)] = ref[rows, 384:].astype(f32)

        @pl.when(pl.program_id(0) == 0)
        def _():
            sums = arrays[0][512:, :].astype(f32)
            for ref in arrays[1:]:
                sums += ref[512:, :].astype(f32)
            for k in range(8):
                vectors[k][...] = sums[k : k + 1, :].reshape(512)
            for k in range(4):
                vectors[8][pl.ds(512 * k, 512)] = sums[8 + k : 9 + k, :].reshape(512)

    vector = pl.BlockSpec((512,), lambda j, t: (0,))
    return stepped(
        body,
        4,
        table,
        arrays,
        [pl.BlockSpec(memory_space=pltpu.VMEM)] * 8,
        [shape((512, 3 * D), f32), shape((512, D), f32)] + [shape((512,), f32)] * 8 + [shape((2048,), f32)],
        [block((128, 3 * D), lambda j, t: (j, 0)), block((128, D), lambda j, t: (j, 0))]
        + [vector] * 8
        + [pl.BlockSpec((2048,), lambda j, t: (0,))],
        cost(6),
        near=True,
    )


def cut(array, start, size, axis):
    return lax.dynamic_slice_in_dim(array, start, size, axis)


def both(upper, lower):
    return jnp.concatenate([upper, lower], 0)


def zero(t):
    return 0


ROUND = ("z", "x", "xz")
DEALT = ("xz", "x", "z")


def send_quarters(quarters):
    return [swap(array, SECOND[name]) for array, name in zip(quarters, DEALT)]


def send_round(array):
    return [swap(array, FIRST[name]) for name in ROUND]


def share(array):
    across = swap(array, FIRST["xz"])
    return [swap(array, FIRST["x"]), swap(array, FIRST["z"]), across]


def arrays_of(found):
    return [piece[0] for piece in found]


def send_dealt(dealt):
    across, over_x, over_z, own = dealt
    across = swap(across, FIRST["xz"])
    over_x = swap(over_x, FIRST["x"])
    over_z = swap(over_z, FIRST["z"])
    return [(array, 0, 0) for array in (own, over_x, over_z, across)]


def shards(
    block_input,
    segment_ids,
    ln1_gain,
    ln1_bias,
    w_qkv,
    b_query,
    b_value,
    w_out,
    b_out,
    ln2_gain,
    ln2_bias,
    w_fc,
    b_fc,
    w_proj,
    b_proj,
    cotangent,
):
    MADE.clear()
    device = lax.axis_index("group") * 64 + lax.axis_index("replica")
    table = lax.dynamic_slice(jnp.asarray(numbers()), (device, 0), (1, NUMBERS)).reshape(NUMBERS)
    c = table[C]

    first, fc_part = pack(
        table, block_input, w_out, w_fc,
        (ln1_gain, ln1_bias, b_query, b_value, b_out, ln2_gain, ln2_bias, b_proj, b_fc),
    )
    early = jnp.concatenate([cotangent, block_input], 1)
    early = both(early, swap(early, CORE))
    earlies = [early, *share(early)]
    out_near = swap(first, FIRST["g"])
    fc_near = swap(after(fc_part, first), FIRST["g"])
    proj_parts = [cut(after(w_proj, first), c * 1024 + 512 * k, 512, 0) for k in range(2)]
    qkv_part = cut(after(w_qkv, first), c * 256, 256, 0)
    part_mine, part_theirs = project(
        after(table, early, proj_parts, qkv_part), first, out_near, ln1_gain, ln1_bias, w_qkv
    )
    part_theirs = swap(part_theirs, FIRST["g"])
    out_far = swap(after(out_near, part_mine), CORE)
    full, fc_bias = spread(after(table, part_mine, out_far, fc_near), first, out_near)
    fc_z = swap(after(fc_near, part_mine), FIRST["z"])
    fc_pair = both(fc_near, fc_z)
    fc_x = swap(fc_pair, FIRST["x"])
    fc_quarters = [fc_near, fc_z, fc_x, fc_x]

    projected, mixture = mix(after(table, fc_pair), part_mine, part_theirs, full, segment_ids)
    proj_first = swap(after(proj_parts[0], part_theirs), FIRST["g"])
    side, residual = settle(after(table, earlies, fc_x, proj_first), mixture, block_input, full, w_out, out_near, out_far)
    proj_second = swap(after(proj_parts[1], part_theirs), FIRST["g"])
    side = both(after(side, proj_second), swap(side, CORE))
    sides = [side, *share(side)]
    qkv_near = swap(after(qkv_part, proj_first), FIRST["g"])

    hidden, grad_pre, fc_sums, back_mine, back_theirs, output_mine, output_theirs, normed_ones = feed_forward(
        table, side, earlies, w_fc, fc_quarters, fc_bias, w_proj, (proj_first, proj_second), full
    )
    back_theirs = swap(back_theirs, CORE)
    feed_dealt = deal_feed(after(table, sides, qkv_near), hidden, grad_pre)
    feeds = send_dealt(feed_dealt)

    grad_residual, dealt, sums = attend_back(
        after(table, feed_dealt), back_mine, back_theirs, residual, cotangent, full,
        projected, segment_ids, w_out, out_near, out_far,
    )
    result = (residual + (output_mine + swap(output_theirs, CORE) + full[7:8])).astype(bf16)
    dealt_theirs = swap(lax.dynamic_index_in_dim(dealt, 1 - c, 0, False), CORE)
    attention_dealt = deal_attention(after(table, arrays_of(feeds)), dealt, dealt_theirs)
    attention_grads = send_dealt(attention_dealt)
    qkv_far = swap(after(qkv_near, attention_dealt), CORE)
    feed_pieces = [
        [(array, 0, 0) for array in sides],
        feeds,
        feeds,
        [(array, 0, 0) for array in earlies],
    ]
    feed_out = feed_sent(after(table, attention_dealt), *feed_pieces)
    feed_received = swap(feed_out, FIRST["g"])
    input_grad, sums = input_back(
        after(table, feed_out), dealt, w_qkv, qkv_near, qkv_far, block_input, grad_residual, full, sums, fc_sums
    )

    normed_pieces = [(normed_ones, row, 0) for row in range(4)]
    out = attention_sent(
        after(table, sums), normed_pieces, [(array, 0, 2) for array in sides], attention_grads, sums
    )
    received = swap(out, FIRST["g"])
    *feed, feed_kept = feed_total(after(table, out), *feed_pieces, feed_received)
    feed = send_quarters(feed)
    sent, kept, sums = attention_total(
        after(table, feed_kept), normed_pieces, [(array, 0, 4) for array in sides], attention_grads, received, sums
    )
    received = swap(sent, SECOND["x"])
    feed = add_up(after(table, kept), feed_kept, feed)
    feed_far = swap(feed, FAR)
    sent, kept, sums = add_split(after(table, feed), kept, received, sums)
    received = swap(sent, SECOND["z"])
    feed = add_up(after(table, kept), feed, [feed_far])
    feed_others = [swap(feed, SECOND[name]) for name in DEALT]
    low = add_low(after(table, feed), kept, received, sums)
    far = swap(low, FAR)
    feed = place_quarters(after(table, low), feed, feed_others)
    feed_z = swap(feed, FIRST["z"])
    feed_x = swap(feed, FIRST["x"])
    low, sums = add_far(after(table, feed), low, far, EXTRA)
    low = place(table, VZ, low, swap(low, SECOND["z"]))
    other = swap(low, SECOND["x"])
    feed_xz = swap(after(feed_z, low), FIRST["x"])
    attention = place(table, VX, low, other, sums)
    attentions = [attention, *send_round(attention)]
    feeds = [feed, feed_z, feed_x, feed_xz]
    feeds += [swap(after(array, attention), CORE) for array in feeds]
    fc_grad, proj_grad = unpack_feed(after(table, attention), feeds)
    attentions = attentions + [swap(array, CORE) for array in attentions]
    qkv_grad, out_grad, *vectors = unpack_attention(after(table, fc_grad), attentions)
    return (
        result,
        input_grad,
        vectors[0],
        vectors[1],
        qkv_grad,
        vectors[2],
        vectors[3],
        out_grad,
        vectors[4],
        vectors[5],
        vectors[6],
        fc_grad,
        vectors[8],
        proj_grad,
        vectors[7],
    )


def solution(mesh):
    rows = P(("group", "replica"), None)
    vector = P("group")
    matrix = P("group", None)
    vectors_in = (vector, vector, matrix, vector, vector, matrix, vector, vector, vector, matrix, vector, matrix, vector)
    return jax.shard_map(
        shards,
        mesh=mesh,
        in_specs=(rows, rows) + vectors_in + (rows,),
        out_specs=(rows, rows) + vectors_in,
        check_vma=False,
    )
```

profile of v0, /device:TPU:1, one launch (start us, length us, event | category | flops | bytes accessed | tf_op | source)
XLA Modules:
  0.0 255.8 jit_solution(9304088158978668278)
XLA Ops:
  6.6 3.4 %shard_map.280 = (bf16[400,1024]{1,0:T(8,128)(2,1)}, bf16[128,2048]{1,0:T(8,128)(2,1)}) custom-call(s32[16]{0:T(128)} %get-tuple-element.184.t, bf16[128,1024]{1,0:T(8,128)(2,1)} %in_ref.5, bf16[512,1024]{1,0:T(8,128)(2,1)} %own.4, bf16[512,4096]{1,0:T(8,128)(2,1)} %refs_12_.1, bf16[512,4096]{1,0:T(8,128)(2,1)} %refs_12_.1, bf16[512]{0:T(512)(128)(2,1)} %gain_ref.1, ...), custom_call_target="tpu_custom_call" | custom-call | bytes 13284000 | tf_op jit(solution)/shard_map/pallas_call | solution.py:142
  10.0 2.8 %collective-permute-start.5 = (bf16[400,1024]{1,0:T(8,128)(2,1)}, bf16[400,1024]{1,0:T(8,128)(2,1)}, u32[]{:S(2)}, u32[]{:S(2)}) collective-permute-start(bf16[400,1024]{1,0:T(8,128)(2,1)} %get-tuple-element.107.own_ref), channel_id=1, source_target_pairs={{0,64},{1,97},{2,66},{3,99},{4,68},{5,101},{6,70},{7,103},{8,72},{... | collective-permute-start | bytes 2457608 | tf_op jit(solution)/shard_map/ppermute | solution.py:62
  16.4 6.0 %collective-permute-start.3 = (bf16[256,2048]{1,0:T(8,128)(2,1)}, bf16[256,2048]{1,0:T(8,128)(2,1)}, u32[]{:S(2)}, u32[]{:S(2)}) collective-permute-start(bf16[256,2048]{1,0:T(8,128)(2,1)} %pad_maximum_fusion.refs_1_.refs_12_), channel_id=1, source_target_pairs={{0,10},{1,31},{2,8},{3,29},{4,14},{5,27},{6,12},{7,25},{8,2},{9,23... | collective-permute-start | bytes 3145736 | tf_op jit(solution)/shard_map/ppermute | solution.py:62
  26.2 5.5 %shard_map.281 = (f32[128,3072]{1,0:T(8,128)S(1)}, bf16[128,3072]{1,0:T(8,128)(2,1)S(1)}) custom-call(s32[16]{0:T(128)S(1)} %copy-done.6, bf16[400,1024]{1,0:T(8,128)(2,1)S(1)} %copy-done.1, bf16[400,1024]{1,0:T(8,128)(2,1)} %collective-permute-done.5.other_ref.a, bf16[512]{0:T(512)(128)(2,1)S(1)} %copy-done.7, bf16[512]{0:T(512)(128)(2,1)S(1)} %copy-done.8, ...), custom_call_target="tpu_custom_call" | custom-call | bytes 29520000 | tf_op jit(solution)/shard_map/pallas_call | solution.py:142
  31.7 2.7 %collective-permute-start.8 = (bf16[128,3072]{1,0:T(8,128)(2,1)S(1)}, bf16[128,3072]{1,0:T(8,128)(2,1)S(1)}, u32[]{:S(2)}, u32[]{:S(2)}) collective-permute-start(bf16[128,3072]{1,0:T(8,128)(2,1)S(1)} %get-tuple-element.114), channel_id=1, source_target_pairs={{0,64},{1,97},{2,66},{3,99},{4,68},{5,101},{6,70},{7,103},{8,72},{... | collective-permute-start | bytes 2359304 | tf_op jit(solution)/shard_map/ppermute | solution.py:62
  38.2 5.7 %collective-permute-done.6.refs_7_ = bf16[128,2048]{1,0:T(8,128)(2,1)S(1)} collective-permute-done((bf16[128,2048]{1,0:T(8,128)(2,1)}, bf16[128,2048]{1,0:T(8,128)(2,1)S(1)}, u32[]{:S(2)}, u32[]{:S(2)}) %collective-permute-start.6) | collective-permute-done | bytes 524320 | tf_op jit(solution)/shard_map/ppermute | solution.py:62
  50.7 3.2 %shard_map.283 = (bf16[128,3072]{1,0:T(8,128)(2,1)S(1)}, bf16[128,1024]{1,0:T(8,128)(2,1)S(1)}) custom-call(s32[16]{0:T(128)S(1)} %copy-done.6, f32[128,3072]{1,0:T(8,128)S(1)} %get-tuple-element.112.mine_ref, bf16[128,3072]{1,0:T(8,128)(2,1)} %copy-done.29, f32[8,1024]{1,0:T(8,128)S(1)} %get-tuple-element.120.full_ref.refs_16_, s32[1,128]{1,0:T(1,128)S(1)} %copy-done.9), custom_call_target="tpu_custom_call" | custom-call | bytes 29889000 | tf_op jit(solution)/shard_map/pallas_call | solution.py:142
  55.1 3.8 %collective-permute-done.1.refs_2_.refs_13_ = bf16[256,2048]{1,0:T(8,128)(2,1)S(1)} collective-permute-done((bf16[256,2048]{1,0:T(8,128)(2,1)}, bf16[256,2048]{1,0:T(8,128)(2,1)S(1)}, u32[]{:S(2)}, u32[]{:S(2)}) %collective-permute-start.1) | collective-permute-done | bytes 1048608 | tf_op jit(solution)/shard_map/ppermute | solution.py:62
  58.9 11.2 %collective-permute-done.7.refs_8_.refs_9_ = bf16[256,2048]{1,0:T(8,128)(2,1)S(1)} collective-permute-done((bf16[256,2048]{1,0:T(8,128)(2,1)S(1)}, bf16[256,2048]{1,0:T(8,128)(2,1)S(1)}, u32[]{:S(2)}, u32[]{:S(2)}) %collective-permute-start.7) | collective-permute-done | bytes 1048608 | tf_op jit(solution)/shard_map/ppermute | solution.py:62
  70.2 3.0 %shard_map.284 = (bf16[128,2048]{1,0:T(8,128)(2,1)S(1)}, f32[128,1024]{1,0:T(8,128)S(1)}) custom-call(s32[16]{0:T(128)S(1)} %copy-done.6, bf16[128,1024]{1,0:T(8,128)(2,1)S(1)} %get-tuple-element.121.mixture_ref, bf16[128,1024]{1,0:T(8,128)(2,1)} %in_ref.5, f32[8,1024]{1,0:T(8,128)S(1)} %get-tuple-element.120.full_ref.refs_16_, bf16[512,1024]{1,0:T(8,128)(2,1)} %own.4, ...), custom_call_target="tpu_custom_call" | custom-call | bytes 11070000 | tf_op jit(solution)/shard_map/pallas_call | solution.py:142
  76.0 3.0 %collective-permute-start.16 = (bf16[256,2048]{1,0:T(8,128)(2,1)}, bf16[256,2048]{1,0:T(8,128)(2,1)}, u32[]{:S(2)}, u32[]{:S(2)}) collective-permute-start(bf16[256,2048]{1,0:T(8,128)(2,1)} %constant_dynamic-update-slice_fusion.4.refs_0_.refs_4_), channel_id=1, source_target_pairs={{0,10},{1,31},{2,8},{3,29},{4,14},{5,27},{6,12},{7,25},{8,2},{9,23... | collective-permute-start | bytes 3145736 | tf_op jit(solution)/shard_map/ppermute | solution.py:62
  81.1 22.2 %shard_map.285 = (bf16[256,2048]{1,0:T(8,128)(2,1)S(1)}, bf16[256,2048]{1,0:T(8,128)(2,1)S(1)}, f32[1,2048]{1,0:T(1,128)S(1)}, f32[128,1024]{1,0:T(8,128)S(1)}, ...) custom-call(s32[16]{0:T(128)S(1)} %copy-done.6, ...), custom_call_target="tpu_custom_call" | custom-call | bytes 84870000 | tf_op jit(solution)/shard_map/pallas_call | solution.py:142
  113.0 5.8 %shard_map.287 = (f32[128,1024]{1,0:T(8,128)S(1)}, bf16[2,128,2048]{2,1,0:T(8,128)(2,1)S(1)}, f32[8,1024]{1,0:T(8,128)S(1)}) custom-call(s32[16]{0:T(128)S(1)} %copy-done.6, f32[128,1024]{1,0:T(8,128)S(1)} %copy-done.5, f32[128,1024]{1,0:T(8,128)} %collective-permute-done.21.theirs_ref, f32[128,1024]{1,0:T(8,128)S(1)} %get-tuple-element.122.res_ref, ...), custom_call_target="tpu_custom_call" | custom-call | bytes 42435000 | tf_op jit(solution)/shard_map/pallas_call | solution.py:142
  119.0 4.0 %collective-permute-done.19.refs_6_.refs_10_ = bf16[256,1024]{1,0:T(8,128)(2,1)S(1)} collective-permute-done((bf16[256,1024]{1,0:T(8,128)(2,1)S(1)}, bf16[256,1024]{1,0:T(8,128)(2,1)S(1)}, u32[]{:S(2)}, u32[]{:S(2)}) %collective-permute-start.19) | collective-permute-done | bytes 524320 | tf_op jit(solution)/shard_map/ppermute | solution.py:62
  124.2 4.1 %shard_map.289 = bf16[512,1024]{1,0:T(8,128)(2,1)S(1)} custom-call(s32[16]{0:T(128)S(1)} %copy-done.6, bf16[256,2048]{1,0:T(8,128)(2,1)} %constant_dynamic-update-slice_fusion.4.refs_0_.refs_4_, bf16[256,2048]{1,0:T(8,128)(2,1)} %collective-permute-done.14.refs_1_.refs_5_, bf16[256,2048]{1,0:T(8,128)(2,1)} %collective-permute-done.15.refs_2_.refs_6_, ...), custom_call_target="tpu_custom_call" | custom-call | bytes 15867000 | tf_op jit(solution)/shard_map/pallas_call | solution.py:142
  136.6 8.9 %shard_map.290 = (f32[128,1024]{1,0:T(8,128)}, f32[32,512]{1,0:T(8,128)S(1)}) custom-call(s32[16]{0:T(128)S(1)} %copy-done.6, bf16[2,128,2048]{2,1,0:T(8,128)(2,1)S(1)} %get-tuple-element.142.mine_ref.grad_ref, bf16[512,3072]{1,0:T(8,128)(2,1)} %own.5, bf16[256,3072]{1,0:T(8,128)(2,1)} %collective-permute-done.17.a, bf16[256,3072]{1,0:T(8,128)(2,1)} %copy-done.22, ...), custom_call_target="tpu_custom_call" | custom-call | bytes 33948000 | tf_op jit(solution)/shard_map/pallas_call | solution.py:142
  146.4 3.0 %shard_map.291 = bf16[528,512]{1,0:T(8,128)(2,1)S(1)} custom-call(s32[16]{0:T(128)S(1)} %copy-done.6, bf16[1024,1024]{1,0:T(8,128)(2,1)S(1)} %copy-done, bf16[1024,1024]{1,0:T(8,128)(2,1)S(1)} %copy-done, bf16[1024,1024]{1,0:T(8,128)(2,1)S(1)} %copy-done, bf16[1024,1024]{1,0:T(8,128)(2,1)S(1)} %copy-done, ...), custom_call_target="tpu_custom_call" | custom-call | bytes 12177000 | tf_op jit(solution)/shard_map/pallas_call | solution.py:142
  151.5 5.7 %shard_map.292 = (bf16[128,1024]{1,0:T(8,128)(2,1)S(1)}, bf16[128,1024]{1,0:T(8,128)(2,1)S(1)}, bf16[128,1024]{1,0:T(8,128)(2,1)S(1)}, f32[128,1024]{1,0:T(8,128)S(1)}) custom-call(s32[16]{0:T(128)S(1)} %copy-done.6, bf16[256,2048]{1,0:T(8,128)(2,1)} %constant_dynamic-update-slice_fusion.4.refs_0_.refs_4_, ...), custom_call_target="tpu_custom_call" | custom-call | bytes 18450000 | tf_op jit(solution)/shard_map/pallas_call | solution.py:142
  160.7 3.7 %shard_map.293 = (bf16[272,512]{1,0:T(8,128)(2,1)S(1)}, f32[256,512]{1,0:T(8,128)S(1)}, f32[16,512]{1,0:T(8,128)S(1)}) custom-call(s32[16]{0:T(128)S(1)} %copy-done.6, bf16[1024,1024]{1,0:T(8,128)(2,1)S(1)} %copy-done, bf16[1024,1024]{1,0:T(8,128)(2,1)S(1)} %copy-done, bf16[1024,1024]{1,0:T(8,128)(2,1)S(1)} %copy-done, bf16[1024,1024]{1,0:T(8,128)(2,1)S(1)} %copy-done, ...), custom_call_target="tpu_custom_call" | custom-call | bytes 14391000 | tf_op jit(solution)/shard_map/pallas_call | solution.py:142
  170.4 4.0 %collective-permute-done.33.refs_0_ = bf16[128,1024]{1,0:T(8,128)(2,1)S(1)} collective-permute-done((bf16[128,1024]{1,0:T(8,128)(2,1)S(1)}, bf16[128,1024]{1,0:T(8,128)(2,1)S(1)}, u32[]{:S(2)}, u32[]{:S(2)}) %collective-permute-start.33) | collective-permute-done | bytes 262176 | tf_op jit(solution)/shard_map/ppermute | solution.py:62
  179.9 5.8 %collective-permute-done.34.received_ref = bf16[144,512]{1,0:T(8,128)(2,1)S(1)} collective-permute-done((bf16[144,512]{1,0:T(8,128)(2,1)S(1)}, bf16[144,512]{1,0:T(8,128)(2,1)S(1)}, u32[]{:S(2)}, u32[]{:S(2)}) %collective-permute-start.34) | collective-permute-done | bytes 147488 | tf_op jit(solution)/shard_map/ppermute | solution.py:62
  186.9 2.8 %collective-permute-start.41 = (bf16[512,1024]{1,0:T(8,128)(2,1)S(1)}, bf16[512,1024]{1,0:T(8,128)(2,1)S(1)}, u32[]{:S(2)}, u32[]{:S(2)}) collective-permute-start(bf16[512,1024]{1,0:T(8,128)(2,1)S(1)} %shard_map.298.refs_0_), channel_id=1, source_target_pairs={{0,2},{1,7},{2,0},{3,5},{4,6},{5,3},{6,4},{7,1},{8,10},{9,15},{10,... | collective-permute-start | bytes 3145736 | tf_op jit(solution)/shard_map/ppermute | solution.py:62
  189.7 5.5 %collective-permute-done.38.received_ref = bf16[144,512]{1,0:T(8,128)(2,1)S(1)} collective-permute-done((bf16[144,512]{1,0:T(8,128)(2,1)S(1)}, bf16[144,512]{1,0:T(8,128)(2,1)S(1)}, u32[]{:S(2)}, u32[]{:S(2)}) %collective-permute-start.38) | collective-permute-done | bytes 147488 | tf_op jit(solution)/shard_map/ppermute | solution.py:62
  197.0 4.1 %collective-permute-done.39.other_ref = bf16[128,512]{1,0:T(8,128)(2,1)S(1)} collective-permute-done((bf16[128,512]{1,0:T(8,128)(2,1)S(1)}, bf16[128,512]{1,0:T(8,128)(2,1)S(1)}, u32[]{:S(2)}, u32[]{:S(2)}) %collective-permute-start.39) | collective-permute-done | bytes 131104 | tf_op jit(solution)/shard_map/ppermute | solution.py:62
  205.8 4.3 %collective-permute-done.40.other_ref = bf16[256,512]{1,0:T(8,128)(2,1)S(1)} collective-permute-done((bf16[256,512]{1,0:T(8,128)(2,1)S(1)}, bf16[256,512]{1,0:T(8,128)(2,1)S(1)}, u32[]{:S(2)}, u32[]{:S(2)}) %collective-permute-start.40) | collective-permute-done | bytes 262176 | tf_op jit(solution)/shard_map/ppermute | solution.py:62
  212.4 8.8 %collective-permute-start.13 = (f32[128,1024]{1,0:T(8,128)S(1)}, f32[128,1024]{1,0:T(8,128)S(1)}, u32[]{:S(2)}, u32[]{:S(2)}) collective-permute-start(f32[128,1024]{1,0:T(8,128)S(1)} %copy-done.11), channel_id=1, source_target_pairs={{0,1},{1,0},{2,3},{3,2},{4,5},{5,4},{6,7},{7,6},{8,9},{9,8},{10,11... | collective-permute-start | bytes 1572872 | tf_op jit(solution)/shard_map/ppermute | solution.py:62
  224.1 5.1 %collective-permute-done.50.refs_3_ = bf16[528,512]{1,0:T(8,128)(2,1)S(1)} collective-permute-done((bf16[528,512]{1,0:T(8,128)(2,1)S(1)}, bf16[528,512]{1,0:T(8,128)(2,1)S(1)}, u32[]{:S(2)}, u32[]{:S(2)}) %collective-permute-start.50) | collective-permute-done | bytes 540704 | tf_op jit(solution)/shard_map/ppermute | solution.py:62
  229.2 4.2 %collective-permute-start.45 = (bf16[512,1024]{1,0:T(8,128)(2,1)S(1)}, bf16[512,1024]{1,0:T(8,128)(2,1)S(1)}, u32[]{:S(2)}, u32[]{:S(2)}) collective-permute-start(bf16[512,1024]{1,0:T(8,128)(2,1)S(1)} %collective-permute-done.41.refs_1_), channel_id=1, source_target_pairs={{0,1},{1,0},{2,3},{3,2},{4,5},{5,4},{6,7},{7,6},{8,9},{9,8},{10,11... | collective-permute-start | bytes 3145736 | tf_op jit(solution)/shard_map/ppermute | solution.py:62
  234.7 4.3 %collective-permute-start.47 = (bf16[512,1024]{1,0:T(8,128)(2,1)S(1)}, bf16[512,1024]{1,0:T(8,128)(2,1)S(1)}, u32[]{:S(2)}, u32[]{:S(2)}) collective-permute-start(bf16[512,1024]{1,0:T(8,128)(2,1)S(1)} %collective-permute-done.43.refs_3_), channel_id=1, source_target_pairs={{0,1},{1,0},{2,3},{3,2},{4,5},{5,4},{6,7},{7,6},{8,9},{9,8},{10,11... | collective-permute-start | bytes 3145736 | tf_op jit(solution)/shard_map/ppermute | solution.py:62
  239.0 3.8 %collective-permute-done.48.refs_1_ = bf16[528,512]{1,0:T(8,128)(2,1)S(1)} collective-permute-done((bf16[528,512]{1,0:T(8,128)(2,1)S(1)}, bf16[528,512]{1,0:T(8,128)(2,1)S(1)}, u32[]{:S(2)}, u32[]{:S(2)}) %collective-permute-start.48) | collective-permute-done | bytes 540704 | tf_op jit(solution)/shard_map/ppermute | solution.py:62
  244.7 6.7 %shard_map.302 = (f32[512,4096]{1,0:T(8,128)}, f32[8,256,1024]{2,1,0:T(8,128)}) custom-call(s32[16]{0:T(128)S(1)} %copy-done.6, bf16[512,1024]{1,0:T(8,128)(2,1)S(1)} %shard_map.298.refs_0_, bf16[512,1024]{1,0:T(8,128)(2,1)S(1)} %collective-permute-done.41.refs_1_, bf16[512,1024]{1,0:T(8,128)(2,1)S(1)} %collective-permute-done.42.refs_2_, ...), custom_call_target="tpu_custom_call" | custom-call | bytes 25830000 | tf_op jit(solution)/shard_map/pallas_call | solution.py:142
  251.4 4.2 %shard_map.303 = (f32[512,3072]{1,0:T(8,128)}, f32[512,1024]{1,0:T(8,128)}, f32[512]{0:T(512)}, f32[512]{0:T(512)}, f32[512]{0:T(512)}, /*index=5*/f32[512]{0:T(...) custom-call(s32[16]{0:T(128)S(1)} %copy-done.6, ...), custom_call_target="tpu_custom_call" | custom-call | bytes 22140000 | tf_op jit(solution)/shard_map/pallas_call | solution.py:142
  (176 shorter events, 80.5 us)
Async XLA Ops:
  10.0 16.1 %collective-permute-start.5 = (bf16[400,1024]{1,0:T(8,128)(2,1)}, bf16[400,1024]{1,0:T(8,128)(2,1)}, u32[]{:S(2)}, u32[]{:S(2)}) collective-permute-start(bf16[400,1024]{1,0:T(8,128)(2,1)} %get-tuple-element.107.own_ref), channel_id=1, source_target_pairs={{0,64},{1,97},{2,66},{3,99},{4,68},{5,101},{6,70},{7,103},{8,72},{... | collective-permute-start | bytes 2457608 | tf_op jit(solution)/shard_map/ppermute | solution.py:62
  12.9 21.6 %collective-permute-start.4 = (bf16[128,2048]{1,0:T(8,128)(2,1)}, bf16[128,2048]{1,0:T(8,128)(2,1)}, u32[]{:S(2)}, u32[]{:S(2)}) collective-permute-start(bf16[128,2048]{1,0:T(8,128)(2,1)} %get-tuple-element.108), channel_id=1, source_target_pairs={{0,64},{1,97},{2,66},{3,99},{4,68},{5,101},{6,70},{7,103},{8,72},{... | collective-permute-start | bytes 1572872 | tf_op jit(solution)/shard_map/ppermute | solution.py:62
  16.4 30.3 %collective-permute-start.3 = (bf16[256,2048]{1,0:T(8,128)(2,1)}, bf16[256,2048]{1,0:T(8,128)(2,1)}, u32[]{:S(2)}, u32[]{:S(2)}) collective-permute-start(bf16[256,2048]{1,0:T(8,128)(2,1)} %pad_maximum_fusion.refs_1_.refs_12_), channel_id=1, source_target_pairs={{0,10},{1,31},{2,8},{3,29},{4,14},{5,27},{6,12},{7,25},{8,2},{9,23... | collective-permute-start | bytes 3145736 | tf_op jit(solution)/shard_map/ppermute | solution.py:62
  31.7 12.7 %collective-permute-start.8 = (bf16[128,3072]{1,0:T(8,128)(2,1)S(1)}, bf16[128,3072]{1,0:T(8,128)(2,1)S(1)}, u32[]{:S(2)}, u32[]{:S(2)}) collective-permute-start(bf16[128,3072]{1,0:T(8,128)(2,1)S(1)} %get-tuple-element.114), channel_id=1, source_target_pairs={{0,64},{1,97},{2,66},{3,99},{4,68},{5,101},{6,70},{7,103},{8,72},{... | collective-permute-start | bytes 2359304 | tf_op jit(solution)/shard_map/ppermute | solution.py:62
  35.1 11.7 %collective-permute-start.10 = (bf16[400,1024]{1,0:T(8,128)(2,1)}, bf16[400,1024]{1,0:T(8,128)(2,1)S(1)}, u32[]{:S(2)}, u32[]{:S(2)}) collective-permute-start(bf16[400,1024]{1,0:T(8,128)(2,1)} %collective-permute-done.5.other_ref.a), channel_id=1, source_target_pairs={{0,1},{1,0},{2,3},{3,2},{4,5},{5,4},{6,7},{7,6},{8,9},{9,8},{10,11... | collective-permute-start | bytes 2457608 | tf_op jit(solution)/shard_map/ppermute | solution.py:62
  35.1 20.0 %collective-permute-start.2 = (bf16[256,2048]{1,0:T(8,128)(2,1)}, bf16[256,2048]{1,0:T(8,128)(2,1)S(1)}, u32[]{:S(2)}, u32[]{:S(2)}) collective-permute-start(bf16[256,2048]{1,0:T(8,128)(2,1)} %pad_maximum_fusion.refs_1_.refs_12_), channel_id=1, source_target_pairs={{0,2},{1,7},{2,0},{3,5},{4,6},{5,3},{6,4},{7,1},{8,10},{9,15},{10,... | collective-permute-start | bytes 3145736 | tf_op jit(solution)/shard_map/ppermute | solution.py:62
  43.9 15.1 %collective-permute-start.1 = (bf16[256,2048]{1,0:T(8,128)(2,1)}, bf16[256,2048]{1,0:T(8,128)(2,1)S(1)}, u32[]{:S(2)}, u32[]{:S(2)}) collective-permute-start(bf16[256,2048]{1,0:T(8,128)(2,1)} %pad_maximum_fusion.refs_1_.refs_12_), channel_id=1, source_target_pairs={{0,8},{1,25},{2,10},{3,27},{4,12},{5,29},{6,14},{7,31},{8,0},{9,17... | collective-permute-start | bytes 3145736 | tf_op jit(solution)/shard_map/ppermute | solution.py:62
  44.4 25.8 %collective-permute-start.7 = (bf16[256,2048]{1,0:T(8,128)(2,1)S(1)}, bf16[256,2048]{1,0:T(8,128)(2,1)S(1)}, u32[]{:S(2)}, u32[]{:S(2)}) collective-permute-start(bf16[256,2048]{1,0:T(8,128)(2,1)S(1)} %constant_dynamic-update-slice_fusion.2), channel_id=1, source_target_pairs={{0,8},{1,25},{2,10},{3,27},{4,12},{5,29},{6,14},{7,31},{8,0},{9,17... | collective-permute-start | bytes 3145736 | tf_op jit(solution)/shard_map/ppermute | solution.py:62
  46.7 23.5 %collective-permute-start.9 = (bf16[512,1024]{1,0:T(8,128)(2,1)S(1)}, bf16[512,1024]{1,0:T(8,128)(2,1)S(1)}, u32[]{:S(2)}, u32[]{:S(2)}) collective-permute-start(bf16[512,1024]{1,0:T(8,128)(2,1)S(1)} %get-tuple-element.115), channel_id=1, source_target_pairs={{0,64},{1,97},{2,66},{3,99},{4,68},{5,101},{6,70},{7,103},{8,72},{... | collective-permute-start | bytes 3145736 | tf_op jit(solution)/shard_map/ppermute | solution.py:62
  46.8 26.7 %collective-permute-start.11 = (bf16[512,1024]{1,0:T(8,128)(2,1)S(1)}, bf16[512,1024]{1,0:T(8,128)(2,1)S(1)}, u32[]{:S(2)}, u32[]{:S(2)}) collective-permute-start(bf16[512,1024]{1,0:T(8,128)(2,1)S(1)} %get-tuple-element.124), channel_id=1, source_target_pairs={{0,64},{1,97},{2,66},{3,99},{4,68},{5,101},{6,70},{7,103},{8,72},{... | collective-permute-start | bytes 3145736 | tf_op jit(solution)/shard_map/ppermute | solution.py:62
  73.3 33.8 %collective-permute-start.17 = (bf16[256,3072]{1,0:T(8,128)(2,1)}, bf16[256,3072]{1,0:T(8,128)(2,1)}, u32[]{:S(2)}, u32[]{:S(2)}) collective-permute-start(bf16[256,3072]{1,0:T(8,128)(2,1)} %constant_dynamic-slice_fusion), channel_id=1, source_target_pairs={{0,64},{1,97},{2,66},{3,99},{4,68},{5,101},{6,70},{7,103},{8,72},{... | collective-permute-start | bytes 4718600 | tf_op jit(solution)/shard_map/ppermute | solution.py:62
  76.0 31.0 %collective-permute-start.16 = (bf16[256,2048]{1,0:T(8,128)(2,1)}, bf16[256,2048]{1,0:T(8,128)(2,1)}, u32[]{:S(2)}, u32[]{:S(2)}) collective-permute-start(bf16[256,2048]{1,0:T(8,128)(2,1)} %constant_dynamic-update-slice_fusion.4.refs_0_.refs_4_), channel_id=1, source_target_pairs={{0,10},{1,31},{2,8},{3,29},{4,14},{5,27},{6,12},{7,25},{8,2},{9,23... | collective-permute-start | bytes 3145736 | tf_op jit(solution)/shard_map/ppermute | solution.py:62
  79.0 28.0 %collective-permute-start.15 = (bf16[256,2048]{1,0:T(8,128)(2,1)}, bf16[256,2048]{1,0:T(8,128)(2,1)}, u32[]{:S(2)}, u32[]{:S(2)}) collective-permute-start(bf16[256,2048]{1,0:T(8,128)(2,1)} %constant_dynamic-update-slice_fusion.4.refs_0_.refs_4_), channel_id=1, source_target_pairs={{0,2},{1,7},{2,0},{3,5},{4,6},{5,3},{6,4},{7,1},{8,10},{9,15},{10,... | collective-permute-start | bytes 3145736 | tf_op jit(solution)/shard_map/ppermute | solution.py:62
  79.1 28.0 %collective-permute-start.14 = (bf16[256,2048]{1,0:T(8,128)(2,1)}, bf16[256,2048]{1,0:T(8,128)(2,1)}, u32[]{:S(2)}, u32[]{:S(2)}) collective-permute-start(bf16[256,2048]{1,0:T(8,128)(2,1)} %constant_dynamic-update-slice_fusion.4.refs_0_.refs_4_), channel_id=1, source_target_pairs={{0,8},{1,25},{2,10},{3,27},{4,12},{5,29},{6,14},{7,31},{8,0},{9,17... | collective-permute-start | bytes 3145736 | tf_op jit(solution)/shard_map/ppermute | solution.py:62
  107.9 11.2 %collective-permute-start.18 = (bf16[256,1024]{1,0:T(8,128)(2,1)S(1)}, bf16[256,1024]{1,0:T(8,128)(2,1)S(1)}, u32[]{:S(2)}, u32[]{:S(2)}) collective-permute-start(bf16[256,1024]{1,0:T(8,128)(2,1)S(1)} %get-tuple-element.134), channel_id=1, source_target_pairs={{0,8},{1,25},{2,10},{3,27},{4,12},{5,29},{6,14},{7,31},{8,0},{9,17... | collective-permute-start | bytes 1572872 | tf_op jit(solution)/shard_map/ppermute | solution.py:62
  108.6 14.4 %collective-permute-start.19 = (bf16[256,1024]{1,0:T(8,128)(2,1)S(1)}, bf16[256,1024]{1,0:T(8,128)(2,1)S(1)}, u32[]{:S(2)}, u32[]{:S(2)}) collective-permute-start(bf16[256,1024]{1,0:T(8,128)(2,1)S(1)} %get-tuple-element.135), channel_id=1, source_target_pairs={{0,2},{1,7},{2,0},{3,5},{4,6},{5,3},{6,4},{7,1},{8,10},{9,15},{10,... | collective-permute-start | bytes 1572872 | tf_op jit(solution)/shard_map/ppermute | solution.py:62
  111.3 12.2 %collective-permute-start.20 = (bf16[256,1024]{1,0:T(8,128)(2,1)S(1)}, bf16[256,1024]{1,0:T(8,128)(2,1)S(1)}, u32[]{:S(2)}, u32[]{:S(2)}) collective-permute-start(bf16[256,1024]{1,0:T(8,128)(2,1)S(1)} %get-tuple-element.136), channel_id=1, source_target_pairs={{0,10},{1,31},{2,8},{3,29},{4,14},{5,27},{6,12},{7,25},{8,2},{9,23... | collective-permute-start | bytes 1572872 | tf_op jit(solution)/shard_map/ppermute | solution.py:62
  124.1 11.4 %collective-permute-start.23 = (bf16[256,3072]{1,0:T(8,128)(2,1)}, bf16[256,3072]{1,0:T(8,128)(2,1)S(1)}, u32[]{:S(2)}, u32[]{:S(2)}) collective-permute-start(bf16[256,3072]{1,0:T(8,128)(2,1)} %collective-permute-done.17.a), channel_id=1, source_target_pairs={{0,1},{1,0},{2,3},{3,2},{4,5},{5,4},{6,7},{7,6},{8,9},{9,8},{10,11... | collective-permute-start | bytes 4718600 | tf_op jit(solution)/shard_map/ppermute | solution.py:62
  128.3 22.2 %collective-permute-start.27 = (bf16[512,1024]{1,0:T(8,128)(2,1)S(1)}, bf16[512,1024]{1,0:T(8,128)(2,1)S(1)}, u32[]{:S(2)}, u32[]{:S(2)}) collective-permute-start(bf16[512,1024]{1,0:T(8,128)(2,1)S(1)} %shard_map.289), channel_id=1, source_target_pairs={{0,64},{1,97},{2,66},{3,99},{4,68},{5,101},{6,70},{7,103},{8,72},{... | collective-permute-start | bytes 3145736 | tf_op jit(solution)/shard_map/ppermute | solution.py:62
  130.4 15.1 %collective-permute-start.26 = (bf16[256,512]{1,0:T(8,128)(2,1)S(1)}, bf16[256,512]{1,0:T(8,128)(2,1)S(1)}, u32[]{:S(2)}, u32[]{:S(2)}) collective-permute-start(bf16[256,512]{1,0:T(8,128)(2,1)S(1)} %get-tuple-element.143), channel_id=1, source_target_pairs={{0,10},{1,31},{2,8},{3,29},{4,14},{5,27},{6,12},{7,25},{8,2},{9,23... | collective-permute-start | bytes 786440 | tf_op jit(solution)/shard_map/ppermute | solution.py:62
  133.1 12.4 %collective-permute-start.24 = (bf16[256,512]{1,0:T(8,128)(2,1)S(1)}, bf16[256,512]{1,0:T(8,128)(2,1)S(1)}, u32[]{:S(2)}, u32[]{:S(2)}) collective-permute-start(bf16[256,512]{1,0:T(8,128)(2,1)S(1)} %get-tuple-element.144), channel_id=1, source_target_pairs={{0,8},{1,25},{2,10},{3,27},{4,12},{5,29},{6,14},{7,31},{8,0},{9,17... | collective-permute-start | bytes 786440 | tf_op jit(solution)/shard_map/ppermute | solution.py:62
  149.4 10.5 %collective-permute-start.28 = (bf16[528,512]{1,0:T(8,128)(2,1)S(1)}, bf16[528,512]{1,0:T(8,128)(2,1)S(1)}, u32[]{:S(2)}, u32[]{:S(2)}) collective-permute-start(bf16[528,512]{1,0:T(8,128)(2,1)S(1)} %shard_map.291), channel_id=1, source_target_pairs={{0,64},{1,97},{2,66},{3,99},{4,68},{5,101},{6,70},{7,103},{8,72},{... | collective-permute-start | bytes 1622024 | tf_op jit(solution)/shard_map/ppermute | solution.py:62
  175.1 11.2 %collective-permute-start.37 = (bf16[128,1024]{1,0:T(8,128)(2,1)S(1)}, bf16[128,1024]{1,0:T(8,128)(2,1)S(1)}, u32[]{:S(2)}, u32[]{:S(2)}) collective-permute-start(bf16[128,1024]{1,0:T(8,128)(2,1)S(1)} %shard_map.296.refs_3_), channel_id=1, source_target_pairs={{0,6},{1,3},{2,4},{3,1},{4,2},{5,7},{6,0},{7,5},{8,14},{9,11},{10,... | collective-permute-start | bytes 786440 | tf_op jit(solution)/shard_map/ppermute | solution.py:62
  186.9 16.6 %collective-permute-start.41 = (bf16[512,1024]{1,0:T(8,128)(2,1)S(1)}, bf16[512,1024]{1,0:T(8,128)(2,1)S(1)}, u32[]{:S(2)}, u32[]{:S(2)}) collective-permute-start(bf16[512,1024]{1,0:T(8,128)(2,1)S(1)} %shard_map.298.refs_0_), channel_id=1, source_target_pairs={{0,2},{1,7},{2,0},{3,5},{4,6},{5,3},{6,4},{7,1},{8,10},{9,15},{10,... | collective-permute-start | bytes 3145736 | tf_op jit(solution)/shard_map/ppermute | solution.py:62
  189.7 33.9 %collective-permute-start.42 = (bf16[512,1024]{1,0:T(8,128)(2,1)S(1)}, bf16[512,1024]{1,0:T(8,128)(2,1)S(1)}, u32[]{:S(2)}, u32[]{:S(2)}) collective-permute-start(bf16[512,1024]{1,0:T(8,128)(2,1)S(1)} %shard_map.298.refs_0_), channel_id=1, source_target_pairs={{0,8},{1,25},{2,10},{3,27},{4,12},{5,29},{6,14},{7,31},{8,0},{9,17... | collective-permute-start | bytes 3145736 | tf_op jit(solution)/shard_map/ppermute | solution.py:62
  203.5 29.9 %collective-permute-start.43 = (bf16[512,1024]{1,0:T(8,128)(2,1)S(1)}, bf16[512,1024]{1,0:T(8,128)(2,1)S(1)}, u32[]{:S(2)}, u32[]{:S(2)}) collective-permute-start(bf16[512,1024]{1,0:T(8,128)(2,1)S(1)} %collective-permute-done.41.refs_1_), channel_id=1, source_target_pairs={{0,8},{1,25},{2,10},{3,27},{4,12},{5,29},{6,14},{7,31},{8,0},{9,17... | collective-permute-start | bytes 3145736 | tf_op jit(solution)/shard_map/ppermute | solution.py:62
  210.7 18.4 %collective-permute-start.50 = (bf16[528,512]{1,0:T(8,128)(2,1)S(1)}, bf16[528,512]{1,0:T(8,128)(2,1)S(1)}, u32[]{:S(2)}, u32[]{:S(2)}) collective-permute-start(bf16[528,512]{1,0:T(8,128)(2,1)S(1)} %shard_map.301.refs_0_), channel_id=1, source_target_pairs={{0,10},{1,31},{2,8},{3,29},{4,14},{5,27},{6,12},{7,25},{8,2},{9,23... | collective-permute-start | bytes 1622024 | tf_op jit(solution)/shard_map/ppermute | solution.py:62
  212.4 11.2 %collective-permute-start.13 = (f32[128,1024]{1,0:T(8,128)S(1)}, f32[128,1024]{1,0:T(8,128)S(1)}, u32[]{:S(2)}, u32[]{:S(2)}) collective-permute-start(f32[128,1024]{1,0:T(8,128)S(1)} %copy-done.11), channel_id=1, source_target_pairs={{0,1},{1,0},{2,3},{3,2},{4,5},{5,4},{6,7},{7,6},{8,9},{9,8},{10,11... | collective-permute-start | bytes 1572872 | tf_op jit(solution)/shard_map/ppermute | solution.py:62
  221.2 13.5 %collective-permute-start.49 = (bf16[528,512]{1,0:T(8,128)(2,1)S(1)}, bf16[528,512]{1,0:T(8,128)(2,1)S(1)}, u32[]{:S(2)}, u32[]{:S(2)}) collective-permute-start(bf16[528,512]{1,0:T(8,128)(2,1)S(1)} %shard_map.301.refs_0_), channel_id=1, source_target_pairs={{0,8},{1,25},{2,10},{3,27},{4,12},{5,29},{6,14},{7,31},{8,0},{9,17... | collective-permute-start | bytes 1622024 | tf_op jit(solution)/shard_map/ppermute | solution.py:62
  223.6 19.2 %collective-permute-start.44 = (bf16[512,1024]{1,0:T(8,128)(2,1)S(1)}, bf16[512,1024]{1,0:T(8,128)(2,1)S(1)}, u32[]{:S(2)}, u32[]{:S(2)}) collective-permute-start(bf16[512,1024]{1,0:T(8,128)(2,1)S(1)} %shard_map.298.refs_0_), channel_id=1, source_target_pairs={{0,1},{1,0},{2,3},{3,2},{4,5},{5,4},{6,7},{7,6},{8,9},{9,8},{10,11... | collective-permute-start | bytes 3145736 | tf_op jit(solution)/shard_map/ppermute | solution.py:62
  223.6 19.7 %collective-permute-start.46 = (bf16[512,1024]{1,0:T(8,128)(2,1)S(1)}, bf16[512,1024]{1,0:T(8,128)(2,1)S(1)}, u32[]{:S(2)}, u32[]{:S(2)}) collective-permute-start(bf16[512,1024]{1,0:T(8,128)(2,1)S(1)} %collective-permute-done.42.refs_2_), channel_id=1, source_target_pairs={{0,1},{1,0},{2,3},{3,2},{4,5},{5,4},{6,7},{7,6},{8,9},{9,8},{10,11... | collective-permute-start | bytes 3145736 | tf_op jit(solution)/shard_map/ppermute | solution.py:62
  229.2 14.2 %collective-permute-start.45 = (bf16[512,1024]{1,0:T(8,128)(2,1)S(1)}, bf16[512,1024]{1,0:T(8,128)(2,1)S(1)}, u32[]{:S(2)}, u32[]{:S(2)}) collective-permute-start(bf16[512,1024]{1,0:T(8,128)(2,1)S(1)} %collective-permute-done.41.refs_1_), channel_id=1, source_target_pairs={{0,1},{1,0},{2,3},{3,2},{4,5},{5,4},{6,7},{7,6},{8,9},{9,8},{10,11... | collective-permute-start | bytes 3145736 | tf_op jit(solution)/shard_map/ppermute | solution.py:62
  (53 other events, 423.2 us)
where the time goes:
time: 257 us; the launch traced here: 256 us
  Pallas kernels  86.9 us (34%)
  starting transfers between devices  79.4 us (31%)
  waiting for transfers between devices  65.1 us (25%)
  local copies, waits for them, and re-layouts  17.3 us (7%)
  between operations  3.97 us (2%)
  other arithmetic  3.11 us (1%)
    pallas_call x24, Pallas kernels, stepped(): pl.pallas_call(body, grid_spec=pltpu.PrefetchScalarGridSpec(num_scalar_pr...  86.9 us
    ppermute x55, starting transfers between devices, swap(): return lax.ppermute(array, AXES, pairs)  79.4 us
    ppermute x55, waiting for transfers between devices, swap(): return lax.ppermute(array, AXES, pairs)  65.1 us
    unnamed x63, local copies, waits for them, and re-layouts  9.87 us
  transfers between devices with their start and end apart: 55, of which 18 were waited for; matrix products, arithmetic and copies ran while one was open for 4% of the time, Pallas kernels for 32%

commit v1 on v0

--- a/solution.py
+++ b/solution.py
@@ -333,116 +333,87 @@
     )
 
 
-def feed_forward(table, side, early, w_fc, quarters, bias, w_proj, others, full):
-    def units(j, t):
-        return jnp.where(j % 4 < 2, t[G], 1 - t[G]) * 2 + j % 2
-
-    def body(t, *refs):
-        side_ref, early_refs, own_fc, pieces_fc = refs[0], refs[1:5], refs[5], refs[6:10]
-        bias_ref, low_ref, high_ref, own_proj, first_proj, second_proj, full_ref = refs[10:17]
-        hidden_ref, grad_ref, sums_ref, back_mine, back_theirs, out_mine, out_theirs, normed_ref, slope_ref = refs[17:]
-        j = pl.program_id(0)
-        k = j % 4
-        columns = span(units(j, t) * 512, 512)
-
-        @pl.when(j < 4)
-        def _():
-            here = span(k * 512, 512)
-            values = dot(side_ref[:, span(t[PIECE], 512)], own_fc[...])
-            for i, ref in enumerate(pieces_fc):
-                values += dot(side_ref[:, span(t[QUARTER + i], 128)], ref[:, here])
-            values += bias_ref[:, here]
+def feed_forward(table, side, early, w_fc, fc_others, bias, w_proj, proj_others):
+    def body(t, side_ref, cot_ref, bias_ref, w_fc, near_fc, z_fc, x_fc, w_proj, first_proj, second_proj, *refs):
+        hidden_ref, grad_ref, sums_ref, back_mine, back_theirs, out_mine, out_theirs = refs[:7]
+        fc_own, fc_rest, proj_own, proj_rest, rest_ref, slope_ref, sems = refs[7:]
+        low, high = span(t[C] * 1024, 1024), span(2048 + t[C] * 1024, 1024)
+        copies = [
+            (w_fc.at[:, low], fc_own.at[:, :1024]),
+            (w_fc.at[:, high], fc_own.at[:, 1024:]),
+            (near_fc, fc_rest.at[:128]),
+            (z_fc, fc_rest.at[128:256]),
+            (x_fc, fc_rest.at[256:]),
+            (w_proj.at[low], proj_own),
+            (first_proj, proj_rest.at[:512]),
+            (second_proj, proj_rest.at[512:]),
+        ]
+        copies = [pltpu.make_async_copy(src, dst, sems.at[k]) for k, (src, dst) in enumerate(copies)]
+        for copy in copies:
+            copy.start()
+        for i in range(4):
+            rest_ref[:, 128 * i : 128 * (i + 1)] = side_ref[:, span(t[QUARTER + i], 128)]
+        own = side_ref[:, span(t[PIECE], 512)]
+        for copy in copies[:5]:
+            copy.wait()
+        for n in range(4):
+            here = slice(512 * n, 512 * (n + 1))
+            values = dot(own, fc_own[:, here]) + dot(rest_ref[...], fc_rest[:, here]) + bias_ref[:, here]
             square = values * values
             inner = jnp.tanh(gelu_factor * values * (1.0 + 0.044715 * square))
             outer = 0.5 * (1.0 + inner)
             hidden_ref[:, here] = (values * outer).astype(bf16)
             slope_ref[:, here] = outer + values * outer * (1.0 - inner) * gelu_factor * (1.0 + 3.0 * 0.044715 * square)
-
-        def with_proj(use):
-            for ref, wanted in ((own_proj, k < 2), (first_proj, k == 2), (second_proj, k == 3)):
-
-                @pl.when(wanted)
-                def _():
-                    use(ref[...])
-
-        @pl.when((j >= 4) & (j < 8))
-        def _():
-            def use(weights):
-                grad = (dot_rows(early_refs[0][:, :D], weights) * slope_ref[:, columns]).astype(bf16)
+        for copy in copies[5:]:
+            copy.wait()
+        for group, weights in ((t[G], proj_own), (1 - t[G], proj_rest)):
+            for n in range(2):
+                columns = span(group * 1024 + n * 512, 512)
+                grad = (dot_rows(cot_ref[...], weights[512 * n : 512 * (n + 1), :]) * slope_ref[:, columns]).astype(bf16)
                 grad_ref[:, columns] = grad
                 sums_ref[:, columns] = over(grad.astype(f32))
-
-            with_proj(use)
-
-        @pl.when((j >= 8) & (j < 12))
-        def _():
-            def use(low, high, first, size):
-                total = dot_rows(grad_ref[:, :1024], low) + dot_rows(grad_ref[:, 1024:], high)
-                back_mine[:, span(first, size)] = total[:ROWS]
-                back_theirs[:, span(first, size)] = total[ROWS:]
-
-            @pl.when(k < 2)
-            def _():
-                use(low_ref[...], high_ref[...], t[G] * 512 + k * 256, 256)
-
-            for step in (2, 3):
-
-                @pl.when(k == step)
-                def _():
-                    for i in (2 * step - 4, 2 * step - 3):
-                        use(pieces_fc[i][:, :1024], pieces_fc[i][:, 1024:], t[QUARTER + i], 128)
-
-        @pl.when((j >= 12) & (j < 16))
-        def _():
-            def use(weights):
-                total = dot(hidden_ref[:, columns], weights)
-
-                @pl.when(k == 0)
-                def _():
-                    out_mine[...] = total[:ROWS]
-                    out_theirs[...] = total[ROWS:]
-
-                @pl.when(k > 0)
-                def _():
-                    out_mine[...] += total[:ROWS]
-                    out_theirs[...] += total[ROWS:]
-
-            with_proj(use)
-
-        for i, ref in enumerate(early_refs):
-
-            @pl.when(j == 16 + i)
-            def _():
-                normal, _ = norm_parts(ref[:, D:].astype(f32))
-                normed_ref[...] = (normal * full_ref[0:1, :] + full_ref[1:2, :]).astype(bf16)
-
-    def back_rows(j):
-        return jnp.clip(j - 8, 0, 1)
-
-    def proj_rows(j, t):
-        return (t[C] * 2 + jnp.where((j == 4) | (j < 4) | (j == 12), 0, 1), 0)
-
+        total = dot_rows(grad_ref[...], fc_own[...])
+        back_mine[:, span(t[PIECE], 512)] = total[:ROWS]
+        back_theirs[:, span(t[PIECE], 512)] = total[ROWS:]
+        total = dot_rows(grad_ref[...], fc_rest[...])
+        for i in range(4):
+            back_mine[:, span(t[QUARTER + i], 128)] = total[:ROWS, 128 * i : 128 * (i + 1)]
+            back_theirs[:, span(t[QUARTER + i], 128)] = total[ROWS:, 128 * i : 128 * (i + 1)]
+        for n in range(2):
+            here = slice(512 * n, 512 * (n + 1))
+            total = dot(hidden_ref[:, span(t[G] * 1024, 1024)], proj_own[:, here])
+            total += dot(hidden_ref[:, span((1 - t[G]) * 1024, 1024)], proj_rest[:, here])
+            out_mine[:, here] = total[:ROWS]
+            out_theirs[:, here] = total[ROWS:]
+
+    anywhere = pl.BlockSpec(memory_space=pl.ANY)
     square = fixed((ROWS, D))
     return stepped(
         body,
-        20,
-        table,
-        (side, *early, w_fc, *quarters, bias, w_fc, w_fc, w_proj, *others, full),
-        [fixed((BOTH, D))]
-        + [fixed((BOTH, 2 * D))] * 4
-        + [block((512, 512), lambda j, t: (0, jnp.minimum(j, 3) // 2 * 4 + t[C] * 2 + jnp.minimum(j, 3) % 2))]
-        + [fixed((128, 2048), row) for row in (0, 0, 0, 1)]
-        + [fixed((1, 2048))]
-        + [block((256, 1024), lambda j, t: (back_rows(j), t[C])), block((256, 1024), lambda j, t: (back_rows(j), 2 + t[C]))]
-        + [block((512, D), proj_rows), fixed((512, D)), fixed((512, D)), fixed((8, D))],
-        [shape((BOTH, 2048), bf16), shape((BOTH, 2048), bf16), shape((1, 2048), f32)]
-        + [shape((ROWS, D), f32)] * 4
-        + [shape((4 * BOTH, D), bf16)],
-        [fixed((BOTH, 2048)), fixed((BOTH, 2048)), fixed((1, 2048)), square, square, square, square]
-        + [block((BOTH, D), lambda j, t: (jnp.clip(j - 16, 0, 3), 0))],
-        cost(23),
-        [pltpu.VMEM((BOTH, 2048), f32)],
+        1,
+        table,
+        (side, early, bias, w_fc, *fc_others, w_proj, *proj_others),
+        [fixed((BOTH, D)), fixed((BOTH, D)), fixed((1, 2048))] + [anywhere] * 7,
+        [shape((BOTH, 2048), bf16), shape((BOTH, 2048), bf16), shape((1, 2048), f32)] + [shape((ROWS, D), f32)] * 4,
+        [fixed((BOTH, 2048)), fixed((BOTH, 2048)), fixed((1, 2048)), square, square, square, square],
+        cost(12),
+        [pltpu.VMEM((512, 2048), bf16)] * 2
+        + [pltpu.VMEM((1024, D), bf16)] * 2
+        + [pltpu.VMEM((BOTH, 512), bf16), pltpu.VMEM((BOTH, 2048), f32), pltpu.SemaphoreType.DMA((8,))],
         limit=48,
+    )
+
+
+def first_norms(table, pieces, full):
+    def body(t, *refs):
+        full_ref, normed_ref = refs[4:]
+        for i, ref in enumerate(refs[:4]):
+            normal, _ = norm_parts(ref[...].astype(f32))
+            normed_ref[i * BOTH : (i + 1) * BOTH, :] = (normal * full_ref[0:1, :] + full_ref[1:2, :]).astype(bf16)
+
+    return stepped(
+        body, 1, table, (*pieces, full), [fixed((BOTH, D), 0, 1)] * 4 + [fixed((8, D))],
+        shape((4 * BOTH, D), bf16), fixed((4 * BOTH, D)), cost(4),
     )
 
 
@@ -596,18 +567,19 @@
     )
 
 
-def deal_attention(table, mine, theirs):
-    def body(t, mine_ref, theirs_ref, *outs):
+def deal_attention(table, mine, theirs, mixtures):
+    def body(t, mine_ref, theirs_ref, mix_ref, *outs):
         for j, out in enumerate(outs):
             away = 3 - j
             columns = span((((away // 2) ^ t[UX]) * 2 + ((away % 2) ^ t[UZ])) * 512, 512)
-            out[:ROWS, :] = mine_ref[0, :, columns]
-            out[ROWS:, :] = theirs_ref[:, columns]
-
-    return stepped(
-        body, 1, table, (mine, theirs),
-        [pl.BlockSpec((1, ROWS, 2048), lambda j, t: (t[C], 0, 0)), fixed((ROWS, 2048))],
-        [shape((BOTH, 512), bf16)] * 4, [fixed((BOTH, 512))] * 4, cost(0.7), near=True,
+            out[:ROWS, :512] = mine_ref[0, :, columns]
+            out[ROWS:, :512] = theirs_ref[:, columns]
+            out[:, 512:] = mix_ref[...]
+
+    return stepped(
+        body, 1, table, (mine, theirs, mixtures),
+        [pl.BlockSpec((1, ROWS, 2048), lambda j, t: (t[C], 0, 0)), fixed((ROWS, 2048)), fixed((BOTH, D))],
+        [shape((BOTH, 512 + D), bf16)] * 4, [fixed((BOTH, 512 + D))] * 4, cost(1), near=True,
     )
 
 
@@ -1017,7 +989,7 @@
     proj_parts = [cut(after(w_proj, first), c * 1024 + 512 * k, 512, 0) for k in range(2)]
     qkv_part = cut(after(w_qkv, first), c * 256, 256, 0)
     part_mine, part_theirs = project(
-        after(table, early, proj_parts, qkv_part), first, out_near, ln1_gain, ln1_bias, w_qkv
+        after(table, early, proj_parts, qkv_part, fc_near), first, out_near, ln1_gain, ln1_bias, w_qkv
     )
     part_theirs = swap(part_theirs, FIRST["g"])
     out_far = swap(after(out_near, part_mine), CORE)
@@ -1025,30 +997,34 @@
     fc_z = swap(after(fc_near, part_mine), FIRST["z"])
     fc_pair = both(fc_near, fc_z)
     fc_x = swap(fc_pair, FIRST["x"])
-    fc_quarters = [fc_near, fc_z, fc_x, fc_x]
+    fc_others = [fc_near, fc_z, fc_x]
 
     projected, mixture = mix(after(table, fc_pair), part_mine, part_theirs, full, segment_ids)
     proj_first = swap(after(proj_parts[0], part_theirs), FIRST["g"])
     side, residual = settle(after(table, earlies, fc_x, proj_first), mixture, block_input, full, w_out, out_near, out_far)
     proj_second = swap(after(proj_parts[1], part_theirs), FIRST["g"])
-    side = both(after(side, proj_second), swap(side, CORE))
-    sides = [side, *share(side)]
+    side_theirs = swap(side, CORE)
+    side = after(side, proj_second)
+    normed_twos = both(side[:, :D], side_theirs[:, :D])
+    mixtures = both(side[:, D:], side_theirs[:, D:])
+    sides = [normed_twos, *share(normed_twos)]
     qkv_near = swap(after(qkv_part, proj_first), FIRST["g"])
 
-    hidden, grad_pre, fc_sums, back_mine, back_theirs, output_mine, output_theirs, normed_ones = feed_forward(
-        table, side, earlies, w_fc, fc_quarters, fc_bias, w_proj, (proj_first, proj_second), full
+    hidden, grad_pre, fc_sums, back_mine, back_theirs, output_mine, output_theirs = feed_forward(
+        table, normed_twos, early, w_fc, fc_others, fc_bias, w_proj, (proj_first, proj_second)
     )
     back_theirs = swap(back_theirs, CORE)
     feed_dealt = deal_feed(after(table, sides, qkv_near), hidden, grad_pre)
     feeds = send_dealt(feed_dealt)
+    normed_ones = first_norms(after(table, feed_dealt), earlies, full)
 
     grad_residual, dealt, sums = attend_back(
-        after(table, feed_dealt), back_mine, back_theirs, residual, cotangent, full,
+        after(table, normed_ones), back_mine, back_theirs, residual, cotangent, full,
         projected, segment_ids, w_out, out_near, out_far,
     )
     result = (residual + (output_mine + swap(output_theirs, CORE) + full[7:8])).astype(bf16)
     dealt_theirs = swap(lax.dynamic_index_in_dim(dealt, 1 - c, 0, False), CORE)
-    attention_dealt = deal_attention(after(table, arrays_of(feeds)), dealt, dealt_theirs)
+    attention_dealt = deal_attention(after(table, arrays_of(feeds)), dealt, dealt_theirs, mixtures)
     attention_grads = send_dealt(attention_dealt)
     qkv_far = swap(after(qkv_near, attention_dealt), CORE)
     feed_pieces = [
@@ -1065,13 +1041,13 @@
 
     normed_pieces = [(normed_ones, row, 0) for row in range(4)]
     out = attention_sent(
-        after(table, sums), normed_pieces, [(array, 0, 2) for array in sides], attention_grads, sums
+        after(table, sums), normed_pieces, [(array, 0, 1) for array, _, _ in attention_grads], attention_grads, sums
     )
     received = swap(out, FIRST["g"])
     *feed, feed_kept = feed_total(after(table, out), *feed_pieces, feed_received)
     feed = send_quarters(feed)
     sent, kept, sums = attention_total(
-        after(table, feed_kept), normed_pieces, [(array, 0, 4) for array in sides], attention_grads, received, sums
+        after(table, feed_kept), normed_pieces, [(array, 0, 2) for array, _, _ in attention_grads], attention_grads, received, sums
     )
     received = swap(sent, SECOND["x"])
     feed = add_up(after(table, kept), feed_kept, feed)

time: 257 us -> 254 us (0.988)
  Pallas kernels: 86.9 us -> 78.2 us
  waiting for transfers between devices: 65.1 us -> 71.3 us
  starting transfers between devices: 79.4 us -> 82.6 us
    pallas_call x24 -> x25, Pallas kernels: 86.9 us -> 78.2 us  [stepped(): pl.pallas_call(body, grid_spec=pltpu.PrefetchScalarGridSpec(num_scalar_pr...]
    ppermute x55, waiting for transfers between devices: 65.1 us -> 71.3 us  [swap(): return lax.ppermute(array, AXES, pairs)]
    ppermute x55, starting transfers between devices: 79.4 us -> 82.6 us  [swap(): return lax.ppermute(array, AXES, pairs)]
    unnamed x63 -> x78, local copies, waits for them, and re-layouts: 9.87 us -> 8.8 us
  transfers between devices with their start and end apart: 55 -> 55, of which waited for: 18 -> 19; matrix products, arithmetic and copies ran while one was open for 4% -> 3% of each run, Pallas kernels for 32% -> 25%
where the time goes in v1:
time: 254 us; the launch traced here: 253 us
  starting transfers between devices  82.6 us (33%)
  Pallas kernels  78.2 us (31%)
  waiting for transfers between devices  71.3 us (28%)
  local copies, waits for them, and re-layouts  15.4 us (6%)
  between operations  4.05 us (2%)
    ppermute x55, starting transfers between devices, swap(): return lax.ppermute(array, AXES, pairs)  82.6 us
    pallas_call x25, Pallas kernels, stepped(): pl.pallas_call(body, grid_spec=pltpu.PrefetchScalarGridSpec(num_scalar_pr...  78.2 us
    ppermute x55, waiting for transfers between devices, swap(): return lax.ppermute(array, AXES, pairs)  71.3 us
    unnamed x78, local copies, waits for them, and re-layouts  8.8 us
  transfers between devices with their start and end apart: 55, of which 19 were waited for; matrix products, arithmetic and copies ran while one was open for 3% of the time, Pallas kernels for 25%

profile of v1, /device:TPU:1, one launch (start us, length us, event | category | flops | bytes accessed | tf_op | source)
XLA Modules:
  0.0 253.2 jit_solution(12211808631086414021)
XLA Ops:
  1.9 3.3 %shard_map.280 = (bf16[400,1024]{1,0:T(8,128)(2,1)}, bf16[128,2048]{1,0:T(8,128)(2,1)}) custom-call(s32[16]{0:T(128)} %get-tuple-element.184.t, bf16[128,1024]{1,0:T(8,128)(2,1)} %in_ref.5, bf16[512,1024]{1,0:T(8,128)(2,1)} %own.4, bf16[512,4096]{1,0:T(8,128)(2,1)} %w_fc.1, bf16[512,4096]{1,0:T(8,128)(2,1)} %w_fc.1, bf16[512]{0:T(512)(128)(2,1)} %gain_ref.1, ...), custom_call_target="tpu_custom_call" | custom-call | bytes 13284000 | tf_op jit(solution)/shard_map/pallas_call | solution.py:142
  5.1 3.6 %collective-permute-start.5 = (bf16[400,1024]{1,0:T(8,128)(2,1)}, bf16[400,1024]{1,0:T(8,128)(2,1)S(1)}, u32[]{:S(2)}, u32[]{:S(2)}) collective-permute-start(bf16[400,1024]{1,0:T(8,128)(2,1)} %get-tuple-element.107.own_ref), channel_id=1, source_target_pairs={{0,64},{1,97},{2,66},{3,99},{4,68},{5,101},{6,70},{7,103},{8,72},{... | collective-permute-start | bytes 2457608 | tf_op jit(solution)/shard_map/ppermute | solution.py:62
  16.0 8.2 %collective-permute-done.4.near_fc = bf16[128,2048]{1,0:T(8,128)(2,1)S(1)} collective-permute-done((bf16[128,2048]{1,0:T(8,128)(2,1)}, bf16[128,2048]{1,0:T(8,128)(2,1)S(1)}, u32[]{:S(2)}, u32[]{:S(2)}) %collective-permute-start.4) | collective-permute-done | bytes 524320 | tf_op jit(solution)/shard_map/ppermute | solution.py:62
  25.2 5.5 %shard_map.281 = (f32[128,3072]{1,0:T(8,128)S(1)}, bf16[128,3072]{1,0:T(8,128)(2,1)S(1)}) custom-call(s32[16]{0:T(128)S(1)} %copy-done.5, bf16[400,1024]{1,0:T(8,128)(2,1)S(1)} %copy-done, bf16[400,1024]{1,0:T(8,128)(2,1)} %copy-done.13, bf16[512]{0:T(512)(128)(2,1)S(1)} %copy-done.6, bf16[512]{0:T(512)(128)(2,1)S(1)} %copy-done.7, bf16[512,3072]{1,0:T(8,128)(2,1)} %own.5), custom_call_target="tpu_custom_call" | custom-call | bytes 29520000 | tf_op jit(solution)/shard_map/pallas_call | solution.py:142
  33.5 6.0 %collective-permute-start.3 = (bf16[256,2048]{1,0:T(8,128)(2,1)S(1)}, bf16[256,2048]{1,0:T(8,128)(2,1)S(1)}, u32[]{:S(2)}, u32[]{:S(2)}) collective-permute-start(bf16[256,2048]{1,0:T(8,128)(2,1)S(1)} %pad_maximum_fusion.cot_ref.refs_0_.refs_12_), channel_id=1, source_target_pairs={{0,10},{1,31},{2,8},{3,29},{4,14},{5,27},{6,12},{7,25},{8,2},{9,23... | collective-permute-start | bytes 3145736 | tf_op jit(solution)/shard_map/ppermute | solution.py:62
  39.5 3.6 %collective-permute-done.8.theirs_ref = bf16[128,3072]{1,0:T(8,128)(2,1)S(1)} collective-permute-done((bf16[128,3072]{1,0:T(8,128)(2,1)S(1)}, bf16[128,3072]{1,0:T(8,128)(2,1)S(1)}, u32[]{:S(2)}, u32[]{:S(2)}) %collective-permute-start.8) | collective-permute-done | bytes 786464 | tf_op jit(solution)/shard_map/ppermute | solution.py:62
  45.7 3.8 %collective-permute-start.6 = (bf16[128,2048]{1,0:T(8,128)(2,1)S(1)}, bf16[128,2048]{1,0:T(8,128)(2,1)S(1)}, u32[]{:S(2)}, u32[]{:S(2)}) collective-permute-start(bf16[128,2048]{1,0:T(8,128)(2,1)S(1)} %collective-permute-done.4.near_fc), channel_id=1, source_target_pairs={{0,2},{1,7},{2,0},{3,5},{4,6},{5,3},{6,4},{7,1},{8,10},{9,15},{10,... | collective-permute-start | bytes 1572872 | tf_op jit(solution)/shard_map/ppermute | solution.py:62
  52.0 5.2 %collective-permute-done.6.z_fc = bf16[128,2048]{1,0:T(8,128)(2,1)S(1)} collective-permute-done((bf16[128,2048]{1,0:T(8,128)(2,1)S(1)}, bf16[128,2048]{1,0:T(8,128)(2,1)S(1)}, u32[]{:S(2)}, u32[]{:S(2)}) %collective-permute-start.6) | collective-permute-done | bytes 524320 | tf_op jit(solution)/shard_map/ppermute | solution.py:62
  63.7 3.2 %shard_map.283 = (bf16[128,3072]{1,0:T(8,128)(2,1)S(1)}, bf16[128,1024]{1,0:T(8,128)(2,1)S(1)}) custom-call(s32[16]{0:T(128)S(1)} %copy-done.5, f32[128,3072]{1,0:T(8,128)S(1)} %get-tuple-element.112.mine_ref, bf16[128,3072]{1,0:T(8,128)(2,1)} %copy-done.37, f32[8,1024]{1,0:T(8,128)S(1)} %get-tuple-element.120.full_ref.refs_4_, s32[1,128]{1,0:T(1,128)S(1)} %copy-done.8), custom_call_target="tpu_custom_call" | custom-call | bytes 29889000 | tf_op jit(solution)/shard_map/pallas_call | solution.py:142
  68.5 7.1 %collective-permute-done.7.x_fc = bf16[256,2048]{1,0:T(8,128)(2,1)S(1)} collective-permute-done((bf16[256,2048]{1,0:T(8,128)(2,1)S(1)}, bf16[256,2048]{1,0:T(8,128)(2,1)S(1)}, u32[]{:S(2)}, u32[]{:S(2)}) %collective-permute-start.7) | collective-permute-done | bytes 1048608 | tf_op jit(solution)/shard_map/ppermute | solution.py:62
  82.0 4.8 %collective-permute-start.16 = (bf16[256,1024]{1,0:T(8,128)(2,1)}, bf16[256,1024]{1,0:T(8,128)(2,1)}, u32[]{:S(2)}, u32[]{:S(2)}) collective-permute-start(bf16[256,1024]{1,0:T(8,128)(2,1)} %pad_maximum_fusion.1.side_ref.refs_0_), channel_id=1, source_target_pairs={{0,10},{1,31},{2,8},{3,29},{4,14},{5,27},{6,12},{7,25},{8,2},{9,23... | collective-permute-start | bytes 1572872 | tf_op jit(solution)/shard_map/ppermute | solution.py:62
  87.2 10.3 %shard_map.285 = (bf16[256,2048]{1,0:T(8,128)(2,1)S(1)}, bf16[256,2048]{1,0:T(8,128)(2,1)S(1)}, f32[1,2048]{1,0:T(1,128)S(1)}, f32[128,1024]{1,0:T(8,128)S(1)}, ...) custom-call(s32[16]{0:T(128)S(1)} %copy-done.5, ...), custom_call_target="tpu_custom_call" | custom-call | bytes 44280000 | tf_op jit(solution)/shard_map/pallas_call | solution.py:142
  107.2 3.5 %shard_map.287.refs_0_.refs_1_.refs_2_.refs_3_ = bf16[1024,1024]{1,0:T(8,128)(2,1)S(1)} custom-call(s32[16]{0:T(128)S(1)} %copy-done.5, bf16[256,2048]{1,0:T(8,128)(2,1)} %copy-done.11, bf16[256,2048]{1,0:T(8,128)(2,1)} %copy-done.20, bf16[256,2048]{1,0:T(8,128)(2,1)} %copy-done.19, bf16[256,2048]{1,0:T(8,128)(2,1)} %copy-done.18, ...), custom_call_target="tpu_custom_call" | custom-call | bytes 14760000 | tf_op jit(solution)/shard_map/pallas_call | solution.py:142
  110.8 5.9 %shard_map.288 = (f32[128,1024]{1,0:T(8,128)S(1)}, bf16[2,128,2048]{2,1,0:T(8,128)(2,1)S(1)}, f32[8,1024]{1,0:T(8,128)S(1)}) custom-call(s32[16]{0:T(128)S(1)} %copy-done.5, f32[128,1024]{1,0:T(8,128)S(1)} %copy-done.4, f32[128,1024]{1,0:T(8,128)} %collective-permute-done.21.theirs_ref, f32[128,1024]{1,0:T(8,128)S(1)} %get-tuple-element.122.res_ref, ...), custom_call_target="tpu_custom_call" | custom-call | bytes 42435000 | tf_op jit(solution)/shard_map/pallas_call | solution.py:142
  120.5 4.2 %collective-permute-start.26 = (bf16[256,1536]{1,0:T(8,128)(2,1)S(1)}, bf16[256,1536]{1,0:T(8,128)(2,1)S(1)}, u32[]{:S(2)}, u32[]{:S(2)}) collective-permute-start(bf16[256,1536]{1,0:T(8,128)(2,1)S(1)} %get-tuple-element.144), channel_id=1, source_target_pairs={{0,10},{1,31},{2,8},{3,29},{4,14},{5,27},{6,12},{7,25},{8,2},{9,23... | collective-permute-start | bytes 2359304 | tf_op jit(solution)/shard_map/ppermute | solution.py:62
  125.6 4.1 %shard_map.290 = bf16[512,1024]{1,0:T(8,128)(2,1)S(1)} custom-call(s32[16]{0:T(128)S(1)} %copy-done.5, bf16[256,1024]{1,0:T(8,128)(2,1)} %pad_maximum_fusion.1.side_ref.refs_0_, bf16[256,1024]{1,0:T(8,128)(2,1)} %collective-permute-done.14.refs_1_, bf16[256,1024]{1,0:T(8,128)(2,1)} %collective-permute-done.15.refs_2_, ...), custom_call_target="tpu_custom_call" | custom-call | bytes 15867000 | tf_op jit(solution)/shard_map/pallas_call | solution.py:142
  131.0 8.8 %shard_map.291 = (f32[128,1024]{1,0:T(8,128)}, f32[32,512]{1,0:T(8,128)S(1)}) custom-call(s32[16]{0:T(128)S(1)} %copy-done.5, bf16[2,128,2048]{2,1,0:T(8,128)(2,1)S(1)} %get-tuple-element.143.mine_ref.grad_ref, bf16[512,3072]{1,0:T(8,128)(2,1)} %own.5, bf16[256,3072]{1,0:T(8,128)(2,1)} %collective-permute-done.17.a, bf16[256,3072]{1,0:T(8,128)(2,1)} %copy-done.29, ...), custom_call_target="tpu_custom_call" | custom-call | bytes 33948000 | tf_op jit(solution)/shard_map/pallas_call | solution.py:142
  139.8 3.6 %collective-permute-done.24.refs_5_.refs_9_ = bf16[256,1536]{1,0:T(8,128)(2,1)S(1)} collective-permute-done((bf16[256,1536]{1,0:T(8,128)(2,1)S(1)}, bf16[256,1536]{1,0:T(8,128)(2,1)S(1)}, u32[]{:S(2)}, u32[]{:S(2)}) %collective-permute-start.24) | collective-permute-done | bytes 786464 | tf_op jit(solution)/shard_map/ppermute | solution.py:62
  145.2 2.9 %shard_map.292 = bf16[528,512]{1,0:T(8,128)(2,1)S(1)} custom-call(s32[16]{0:T(128)S(1)} %copy-done.5, bf16[1024,1024]{1,0:T(8,128)(2,1)S(1)} %shard_map.287.refs_0_.refs_1_.refs_2_.refs_3_, bf16[1024,1024]{1,0:T(8,128)(2,1)S(1)} %shard_map.287.refs_0_.refs_1_.refs_2_.refs_3_, bf16[1024,1024]{1,0:T(8,128)(2,1)S(1)} %shard_map.287.refs_0_.refs_1_.refs_2_.refs_3_, ...), custom_call_target="tpu_custom_call" | custom-call | bytes 12177000 | tf_op jit(solution)/shard_map/pallas_call | solution.py:142
  149.3 5.6 %shard_map.293 = (bf16[128,1024]{1,0:T(8,128)(2,1)S(1)}, bf16[128,1024]{1,0:T(8,128)(2,1)S(1)}, bf16[128,1024]{1,0:T(8,128)(2,1)S(1)}, f32[128,1024]{1,0:T(8,128)S(1)}) custom-call(s32[16]{0:T(128)S(1)} %copy-done.5, bf16[256,1024]{1,0:T(8,128)(2,1)} %pad_maximum_fusion.1.side_ref.refs_0_, bf16[256,1024]{1,0:T(8,128)(2,1)} %collective-permute-done.14.refs_1_, ...), custom_call_target="tpu_custom_call" | custom-call | bytes 18450000 | tf_op jit(solution)/shard_map/pallas_call | solution.py:142
  158.4 3.6 %shard_map.294 = (bf16[272,512]{1,0:T(8,128)(2,1)S(1)}, f32[256,512]{1,0:T(8,128)S(1)}, f32[16,512]{1,0:T(8,128)S(1)}) custom-call(s32[16]{0:T(128)S(1)} %copy-done.5, bf16[1024,1024]{1,0:T(8,128)(2,1)S(1)} %shard_map.287.refs_0_.refs_1_.refs_2_.refs_3_, bf16[1024,1024]{1,0:T(8,128)(2,1)S(1)} %shard_map.287.refs_0_.refs_1_.refs_2_.refs_3_, ...), custom_call_target="tpu_custom_call" | custom-call | bytes 14391000 | tf_op jit(solution)/shard_map/pallas_call | solution.py:142
  168.4 3.9 %collective-permute-done.33.refs_0_ = bf16[128,1024]{1,0:T(8,128)(2,1)S(1)} collective-permute-done((bf16[128,1024]{1,0:T(8,128)(2,1)S(1)}, bf16[128,1024]{1,0:T(8,128)(2,1)S(1)}, u32[]{:S(2)}, u32[]{:S(2)}) %collective-permute-start.33) | collective-permute-done | bytes 262176 | tf_op jit(solution)/shard_map/ppermute | solution.py:62
  176.2 6.8 %collective-permute-done.34.received_ref = bf16[144,512]{1,0:T(8,128)(2,1)S(1)} collective-permute-done((bf16[144,512]{1,0:T(8,128)(2,1)S(1)}, bf16[144,512]{1,0:T(8,128)(2,1)S(1)}, u32[]{:S(2)}, u32[]{:S(2)}) %collective-permute-start.34) | collective-permute-done | bytes 147488 | tf_op jit(solution)/shard_map/ppermute | solution.py:62
  187.9 3.6 %collective-permute-done.38.received_ref = bf16[144,512]{1,0:T(8,128)(2,1)S(1)} collective-permute-done((bf16[144,512]{1,0:T(8,128)(2,1)S(1)}, bf16[144,512]{1,0:T(8,128)(2,1)S(1)}, u32[]{:S(2)}, u32[]{:S(2)}) %collective-permute-start.38) | collective-permute-done | bytes 147488 | tf_op jit(solution)/shard_map/ppermute | solution.py:62
  192.2 3.7 %collective-permute-done.39.other_ref = bf16[128,512]{1,0:T(8,128)(2,1)S(1)} collective-permute-done((bf16[128,512]{1,0:T(8,128)(2,1)S(1)}, bf16[128,512]{1,0:T(8,128)(2,1)S(1)}, u32[]{:S(2)}, u32[]{:S(2)}) %collective-permute-start.39) | collective-permute-done | bytes 131104 | tf_op jit(solution)/shard_map/ppermute | solution.py:62
  208.3 10.5 %collective-permute-start.13 = (f32[128,1024]{1,0:T(8,128)S(1)}, f32[128,1024]{1,0:T(8,128)S(1)}, u32[]{:S(2)}, u32[]{:S(2)}) collective-permute-start(f32[128,1024]{1,0:T(8,128)S(1)} %copy-done.10), channel_id=1, source_target_pairs={{0,1},{1,0},{2,3},{3,2},{4,5},{5,4},{6,7},{7,6},{8,9},{9,8},{10,11... | collective-permute-start | bytes 1572872 | tf_op jit(solution)/shard_map/ppermute | solution.py:62
  221.0 5.0 %collective-permute-done.50.refs_3_ = bf16[528,512]{1,0:T(8,128)(2,1)S(1)} collective-permute-done((bf16[528,512]{1,0:T(8,128)(2,1)S(1)}, bf16[528,512]{1,0:T(8,128)(2,1)S(1)}, u32[]{:S(2)}, u32[]{:S(2)}) %collective-permute-start.50) | collective-permute-done | bytes 540704 | tf_op jit(solution)/shard_map/ppermute | solution.py:62
  226.1 4.7 %collective-permute-start.45 = (bf16[512,1024]{1,0:T(8,128)(2,1)S(1)}, bf16[512,1024]{1,0:T(8,128)(2,1)S(1)}, u32[]{:S(2)}, u32[]{:S(2)}) collective-permute-start(bf16[512,1024]{1,0:T(8,128)(2,1)S(1)} %collective-permute-done.41.refs_1_), channel_id=1, source_target_pairs={{0,1},{1,0},{2,3},{3,2},{4,5},{5,4},{6,7},{7,6},{8,9},{9,8},{10,11... | collective-permute-start | bytes 3145736 | tf_op jit(solution)/shard_map/ppermute | solution.py:62
  232.7 3.2 %collective-permute-start.47 = (bf16[512,1024]{1,0:T(8,128)(2,1)S(1)}, bf16[512,1024]{1,0:T(8,128)(2,1)S(1)}, u32[]{:S(2)}, u32[]{:S(2)}) collective-permute-start(bf16[512,1024]{1,0:T(8,128)(2,1)S(1)} %collective-permute-done.43.refs_3_), channel_id=1, source_target_pairs={{0,1},{1,0},{2,3},{3,2},{4,5},{5,4},{6,7},{7,6},{8,9},{9,8},{10,11... | collective-permute-start | bytes 3145736 | tf_op jit(solution)/shard_map/ppermute | solution.py:62
  236.0 4.2 %collective-permute-done.48.refs_1_ = bf16[528,512]{1,0:T(8,128)(2,1)S(1)} collective-permute-done((bf16[528,512]{1,0:T(8,128)(2,1)S(1)}, bf16[528,512]{1,0:T(8,128)(2,1)S(1)}, u32[]{:S(2)}, u32[]{:S(2)}) %collective-permute-start.48) | collective-permute-done | bytes 540704 | tf_op jit(solution)/shard_map/ppermute | solution.py:62
  242.0 6.7 %shard_map.303 = (f32[512,4096]{1,0:T(8,128)}, f32[8,256,1024]{2,1,0:T(8,128)}) custom-call(s32[16]{0:T(128)S(1)} %copy-done.5, bf16[512,1024]{1,0:T(8,128)(2,1)S(1)} %shard_map.299.refs_0_, bf16[512,1024]{1,0:T(8,128)(2,1)S(1)} %collective-permute-done.41.refs_1_, bf16[512,1024]{1,0:T(8,128)(2,1)S(1)} %collective-permute-done.42.refs_2_, ...), custom_call_target="tpu_custom_call" | custom-call | bytes 25830000 | tf_op jit(solution)/shard_map/pallas_call | solution.py:142
  248.8 4.2 %shard_map.304 = (f32[512,3072]{1,0:T(8,128)}, f32[512,1024]{1,0:T(8,128)}, f32[512]{0:T(512)}, f32[512]{0:T(512)}, f32[512]{0:T(512)}, /*index=5*/f32[512]{0:T(...) custom-call(s32[16]{0:T(128)S(1)} %copy-done.5, ...), custom_call_target="tpu_custom_call" | custom-call | bytes 22140000 | tf_op jit(solution)/shard_map/pallas_call | solution.py:142
  (195 shorter events, 85.8 us)
Async XLA Ops:
  5.1 19.1 %collective-permute-start.5 = (bf16[400,1024]{1,0:T(8,128)(2,1)}, bf16[400,1024]{1,0:T(8,128)(2,1)S(1)}, u32[]{:S(2)}, u32[]{:S(2)}) collective-permute-start(bf16[400,1024]{1,0:T(8,128)(2,1)} %get-tuple-element.107.own_ref), channel_id=1, source_target_pairs={{0,64},{1,97},{2,66},{3,99},{4,68},{5,101},{6,70},{7,103},{8,72},{... | collective-permute-start | bytes 2457608 | tf_op jit(solution)/shard_map/ppermute | solution.py:62
  8.9 15.4 %collective-permute-start.4 = (bf16[128,2048]{1,0:T(8,128)(2,1)}, bf16[128,2048]{1,0:T(8,128)(2,1)S(1)}, u32[]{:S(2)}, u32[]{:S(2)}) collective-permute-start(bf16[128,2048]{1,0:T(8,128)(2,1)} %get-tuple-element.108), channel_id=1, source_target_pairs={{0,64},{1,97},{2,66},{3,99},{4,68},{5,101},{6,70},{7,103},{8,72},{... | collective-permute-start | bytes 1572872 | tf_op jit(solution)/shard_map/ppermute | solution.py:62
  30.8 12.3 %collective-permute-start.8 = (bf16[128,3072]{1,0:T(8,128)(2,1)S(1)}, bf16[128,3072]{1,0:T(8,128)(2,1)S(1)}, u32[]{:S(2)}, u32[]{:S(2)}) collective-permute-start(bf16[128,3072]{1,0:T(8,128)(2,1)S(1)} %get-tuple-element.114), channel_id=1, source_target_pairs={{0,64},{1,97},{2,66},{3,99},{4,68},{5,101},{6,70},{7,103},{8,72},{... | collective-permute-start | bytes 2359304 | tf_op jit(solution)/shard_map/ppermute | solution.py:62
  33.5 25.8 %collective-permute-start.3 = (bf16[256,2048]{1,0:T(8,128)(2,1)S(1)}, bf16[256,2048]{1,0:T(8,128)(2,1)S(1)}, u32[]{:S(2)}, u32[]{:S(2)}) collective-permute-start(bf16[256,2048]{1,0:T(8,128)(2,1)S(1)} %pad_maximum_fusion.cot_ref.refs_0_.refs_12_), channel_id=1, source_target_pairs={{0,10},{1,31},{2,8},{3,29},{4,14},{5,27},{6,12},{7,25},{8,2},{9,23... | collective-permute-start | bytes 3145736 | tf_op jit(solution)/shard_map/ppermute | solution.py:62
  43.0 16.4 %collective-permute-start.9 = (bf16[512,1024]{1,0:T(8,128)(2,1)S(1)}, bf16[512,1024]{1,0:T(8,128)(2,1)S(1)}, u32[]{:S(2)}, u32[]{:S(2)}) collective-permute-start(bf16[512,1024]{1,0:T(8,128)(2,1)S(1)} %get-tuple-element.115), channel_id=1, source_target_pairs={{0,64},{1,97},{2,66},{3,99},{4,68},{5,101},{6,70},{7,103},{8,72},{... | collective-permute-start | bytes 3145736 | tf_op jit(solution)/shard_map/ppermute | solution.py:62
  45.7 11.6 %collective-permute-start.6 = (bf16[128,2048]{1,0:T(8,128)(2,1)S(1)}, bf16[128,2048]{1,0:T(8,128)(2,1)S(1)}, u32[]{:S(2)}, u32[]{:S(2)}) collective-permute-start(bf16[128,2048]{1,0:T(8,128)(2,1)S(1)} %collective-permute-done.4.near_fc), channel_id=1, source_target_pairs={{0,2},{1,7},{2,0},{3,5},{4,6},{5,3},{6,4},{7,1},{8,10},{9,15},{10,... | collective-permute-start | bytes 1572872 | tf_op jit(solution)/shard_map/ppermute | solution.py:62
  49.5 19.0 %collective-permute-start.2 = (bf16[256,2048]{1,0:T(8,128)(2,1)S(1)}, bf16[256,2048]{1,0:T(8,128)(2,1)S(1)}, u32[]{:S(2)}, u32[]{:S(2)}) collective-permute-start(bf16[256,2048]{1,0:T(8,128)(2,1)S(1)} %pad_maximum_fusion.cot_ref.refs_0_.refs_12_), channel_id=1, source_target_pairs={{0,2},{1,7},{2,0},{3,5},{4,6},{5,3},{6,4},{7,1},{8,10},{9,15},{10,... | collective-permute-start | bytes 3145736 | tf_op jit(solution)/shard_map/ppermute | solution.py:62
  49.5 19.0 %collective-permute-start.1 = (bf16[256,2048]{1,0:T(8,128)(2,1)S(1)}, bf16[256,2048]{1,0:T(8,128)(2,1)S(1)}, u32[]{:S(2)}, u32[]{:S(2)}) collective-permute-start(bf16[256,2048]{1,0:T(8,128)(2,1)S(1)} %pad_maximum_fusion.cot_ref.refs_0_.refs_12_), channel_id=1, source_target_pairs={{0,8},{1,25},{2,10},{3,27},{4,12},{5,29},{6,14},{7,31},{8,0},{9,17... | collective-permute-start | bytes 3145736 | tf_op jit(solution)/shard_map/ppermute | solution.py:62
  57.3 18.3 %collective-permute-start.7 = (bf16[256,2048]{1,0:T(8,128)(2,1)S(1)}, bf16[256,2048]{1,0:T(8,128)(2,1)S(1)}, u32[]{:S(2)}, u32[]{:S(2)}) collective-permute-start(bf16[256,2048]{1,0:T(8,128)(2,1)S(1)} %constant_dynamic-update-slice_fusion.2), channel_id=1, source_target_pairs={{0,8},{1,25},{2,10},{3,27},{4,12},{5,29},{6,14},{7,31},{8,0},{9,17... | collective-permute-start | bytes 3145736 | tf_op jit(solution)/shard_map/ppermute | solution.py:62
  59.5 19.1 %collective-permute-start.11 = (bf16[512,1024]{1,0:T(8,128)(2,1)S(1)}, bf16[512,1024]{1,0:T(8,128)(2,1)S(1)}, u32[]{:S(2)}, u32[]{:S(2)}) collective-permute-start(bf16[512,1024]{1,0:T(8,128)(2,1)S(1)} %get-tuple-element.124), channel_id=1, source_target_pairs={{0,64},{1,97},{2,66},{3,99},{4,68},{5,101},{6,70},{7,103},{8,72},{... | collective-permute-start | bytes 3145736 | tf_op jit(solution)/shard_map/ppermute | solution.py:62
  61.8 39.4 %collective-permute-start.17 = (bf16[256,3072]{1,0:T(8,128)(2,1)}, bf16[256,3072]{1,0:T(8,128)(2,1)}, u32[]{:S(2)}, u32[]{:S(2)}) collective-permute-start(bf16[256,3072]{1,0:T(8,128)(2,1)} %constant_dynamic-slice_fusion), channel_id=1, source_target_pairs={{0,64},{1,97},{2,66},{3,99},{4,68},{5,101},{6,70},{7,103},{8,72},{... | collective-permute-start | bytes 4718600 | tf_op jit(solution)/shard_map/ppermute | solution.py:62
  82.0 19.2 %collective-permute-start.16 = (bf16[256,1024]{1,0:T(8,128)(2,1)}, bf16[256,1024]{1,0:T(8,128)(2,1)}, u32[]{:S(2)}, u32[]{:S(2)}) collective-permute-start(bf16[256,1024]{1,0:T(8,128)(2,1)} %pad_maximum_fusion.1.side_ref.refs_0_), channel_id=1, source_target_pairs={{0,10},{1,31},{2,8},{3,29},{4,14},{5,27},{6,12},{7,25},{8,2},{9,23... | collective-permute-start | bytes 1572872 | tf_op jit(solution)/shard_map/ppermute | solution.py:62
  86.9 14.3 %collective-permute-start.15 = (bf16[256,1024]{1,0:T(8,128)(2,1)}, bf16[256,1024]{1,0:T(8,128)(2,1)}, u32[]{:S(2)}, u32[]{:S(2)}) collective-permute-start(bf16[256,1024]{1,0:T(8,128)(2,1)} %pad_maximum_fusion.1.side_ref.refs_0_), channel_id=1, source_target_pairs={{0,2},{1,7},{2,0},{3,5},{4,6},{5,3},{6,4},{7,1},{8,10},{9,15},{10,... | collective-permute-start | bytes 1572872 | tf_op jit(solution)/shard_map/ppermute | solution.py:62
  86.9 14.3 %collective-permute-start.14 = (bf16[256,1024]{1,0:T(8,128)(2,1)}, bf16[256,1024]{1,0:T(8,128)(2,1)}, u32[]{:S(2)}, u32[]{:S(2)}) collective-permute-start(bf16[256,1024]{1,0:T(8,128)(2,1)} %pad_maximum_fusion.1.side_ref.refs_0_), channel_id=1, source_target_pairs={{0,8},{1,25},{2,10},{3,27},{4,12},{5,29},{6,14},{7,31},{8,0},{9,17... | collective-permute-start | bytes 1572872 | tf_op jit(solution)/shard_map/ppermute | solution.py:62
  99.9 10.8 %collective-permute-start.21 = (f32[128,1024]{1,0:T(8,128)}, f32[128,1024]{1,0:T(8,128)}, u32[]{:S(2)}, u32[]{:S(2)}) collective-permute-start(f32[128,1024]{1,0:T(8,128)} %get-tuple-element.141), channel_id=1, source_target_pairs={{0,1},{1,0},{2,3},{3,2},{4,5},{5,4},{6,7},{7,6},{8,9},{9,8},{10,11... | collective-permute-start | bytes 1572872 | tf_op jit(solution)/shard_map/ppermute | solution.py:62
  102.0 14.8 %collective-permute-start.18 = (bf16[256,1024]{1,0:T(8,128)(2,1)S(1)}, bf16[256,1024]{1,0:T(8,128)(2,1)S(1)}, u32[]{:S(2)}, u32[]{:S(2)}) collective-permute-start(bf16[256,1024]{1,0:T(8,128)(2,1)S(1)} %get-tuple-element.134), channel_id=1, source_target_pairs={{0,8},{1,25},{2,10},{3,27},{4,12},{5,29},{6,14},{7,31},{8,0},{9,17... | collective-permute-start | bytes 1572872 | tf_op jit(solution)/shard_map/ppermute | solution.py:62
  104.5 14.9 %collective-permute-start.19 = (bf16[256,1024]{1,0:T(8,128)(2,1)S(1)}, bf16[256,1024]{1,0:T(8,128)(2,1)S(1)}, u32[]{:S(2)}, u32[]{:S(2)}) collective-permute-start(bf16[256,1024]{1,0:T(8,128)(2,1)S(1)} %get-tuple-element.135), channel_id=1, source_target_pairs={{0,2},{1,7},{2,0},{3,5},{4,6},{5,3},{6,4},{7,1},{8,10},{9,15},{10,... | collective-permute-start | bytes 1572872 | tf_op jit(solution)/shard_map/ppermute | solution.py:62
  107.2 12.2 %collective-permute-start.20 = (bf16[256,1024]{1,0:T(8,128)(2,1)S(1)}, bf16[256,1024]{1,0:T(8,128)(2,1)S(1)}, u32[]{:S(2)}, u32[]{:S(2)}) collective-permute-start(bf16[256,1024]{1,0:T(8,128)(2,1)S(1)} %get-tuple-element.136), channel_id=1, source_target_pairs={{0,10},{1,31},{2,8},{3,29},{4,14},{5,27},{6,12},{7,25},{8,2},{9,23... | collective-permute-start | bytes 1572872 | tf_op jit(solution)/shard_map/ppermute | solution.py:62
  120.5 19.4 %collective-permute-start.26 = (bf16[256,1536]{1,0:T(8,128)(2,1)S(1)}, bf16[256,1536]{1,0:T(8,128)(2,1)S(1)}, u32[]{:S(2)}, u32[]{:S(2)}) collective-permute-start(bf16[256,1536]{1,0:T(8,128)(2,1)S(1)} %get-tuple-element.144), channel_id=1, source_target_pairs={{0,10},{1,31},{2,8},{3,29},{4,14},{5,27},{6,12},{7,25},{8,2},{9,23... | collective-permute-start | bytes 2359304 | tf_op jit(solution)/shard_map/ppermute | solution.py:62
  124.7 18.8 %collective-permute-start.24 = (bf16[256,1536]{1,0:T(8,128)(2,1)S(1)}, bf16[256,1536]{1,0:T(8,128)(2,1)S(1)}, u32[]{:S(2)}, u32[]{:S(2)}) collective-permute-start(bf16[256,1536]{1,0:T(8,128)(2,1)S(1)} %get-tuple-element.145), channel_id=1, source_target_pairs={{0,8},{1,25},{2,10},{3,27},{4,12},{5,29},{6,14},{7,31},{8,0},{9,17... | collective-permute-start | bytes 2359304 | tf_op jit(solution)/shard_map/ppermute | solution.py:62
  125.6 17.8 %collective-permute-start.25 = (bf16[256,1536]{1,0:T(8,128)(2,1)S(1)}, bf16[256,1536]{1,0:T(8,128)(2,1)S(1)}, u32[]{:S(2)}, u32[]{:S(2)}) collective-permute-start(bf16[256,1536]{1,0:T(8,128)(2,1)S(1)} %get-tuple-element.146), channel_id=1, source_target_pairs={{0,2},{1,7},{2,0},{3,5},{4,6},{5,3},{6,4},{7,1},{8,10},{9,15},{10,... | collective-permute-start | bytes 2359304 | tf_op jit(solution)/shard_map/ppermute | solution.py:62
  129.7 18.6 %collective-permute-start.27 = (bf16[512,1024]{1,0:T(8,128)(2,1)S(1)}, bf16[512,1024]{1,0:T(8,128)(2,1)S(1)}, u32[]{:S(2)}, u32[]{:S(2)}) collective-permute-start(bf16[512,1024]{1,0:T(8,128)(2,1)S(1)} %shard_map.290), channel_id=1, source_target_pairs={{0,64},{1,97},{2,66},{3,99},{4,68},{5,101},{6,70},{7,103},{8,72},{... | collective-permute-start | bytes 3145736 | tf_op jit(solution)/shard_map/ppermute | solution.py:62
  173.0 10.6 %collective-permute-start.37 = (bf16[128,1024]{1,0:T(8,128)(2,1)S(1)}, bf16[128,1024]{1,0:T(8,128)(2,1)S(1)}, u32[]{:S(2)}, u32[]{:S(2)}) collective-permute-start(bf16[128,1024]{1,0:T(8,128)(2,1)S(1)} %shard_map.297.refs_3_), channel_id=1, source_target_pairs={{0,6},{1,3},{2,4},{3,1},{4,2},{5,7},{6,0},{7,5},{8,14},{9,11},{10,... | collective-permute-start | bytes 786440 | tf_op jit(solution)/shard_map/ppermute | solution.py:62
  184.2 17.3 %collective-permute-start.41 = (bf16[512,1024]{1,0:T(8,128)(2,1)S(1)}, bf16[512,1024]{1,0:T(8,128)(2,1)S(1)}, u32[]{:S(2)}, u32[]{:S(2)}) collective-permute-start(bf16[512,1024]{1,0:T(8,128)(2,1)S(1)} %shard_map.299.refs_0_), channel_id=1, source_target_pairs={{0,2},{1,7},{2,0},{3,5},{4,6},{5,3},{6,4},{7,1},{8,10},{9,15},{10,... | collective-permute-start | bytes 3145736 | tf_op jit(solution)/shard_map/ppermute | solution.py:62
  186.1 34.4 %collective-permute-start.42 = (bf16[512,1024]{1,0:T(8,128)(2,1)S(1)}, bf16[512,1024]{1,0:T(8,128)(2,1)S(1)}, u32[]{:S(2)}, u32[]{:S(2)}) collective-permute-start(bf16[512,1024]{1,0:T(8,128)(2,1)S(1)} %shard_map.299.refs_0_), channel_id=1, source_target_pairs={{0,8},{1,25},{2,10},{3,27},{4,12},{5,29},{6,14},{7,31},{8,0},{9,17... | collective-permute-start | bytes 3145736 | tf_op jit(solution)/shard_map/ppermute | solution.py:62
  201.5 29.3 %collective-permute-start.43 = (bf16[512,1024]{1,0:T(8,128)(2,1)S(1)}, bf16[512,1024]{1,0:T(8,128)(2,1)S(1)}, u32[]{:S(2)}, u32[]{:S(2)}) collective-permute-start(bf16[512,1024]{1,0:T(8,128)(2,1)S(1)} %collective-permute-done.41.refs_1_), channel_id=1, source_target_pairs={{0,8},{1,25},{2,10},{3,27},{4,12},{5,29},{6,14},{7,31},{8,0},{9,17... | collective-permute-start | bytes 3145736 | tf_op jit(solution)/shard_map/ppermute | solution.py:62
  206.1 20.0 %collective-permute-start.50 = (bf16[528,512]{1,0:T(8,128)(2,1)S(1)}, bf16[528,512]{1,0:T(8,128)(2,1)S(1)}, u32[]{:S(2)}, u32[]{:S(2)}) collective-permute-start(bf16[528,512]{1,0:T(8,128)(2,1)S(1)} %shard_map.302.refs_0_), channel_id=1, source_target_pairs={{0,10},{1,31},{2,8},{3,29},{4,14},{5,27},{6,12},{7,25},{8,2},{9,23... | collective-permute-start | bytes 1622024 | tf_op jit(solution)/shard_map/ppermute | solution.py:62
  208.3 12.6 %collective-permute-start.13 = (f32[128,1024]{1,0:T(8,128)S(1)}, f32[128,1024]{1,0:T(8,128)S(1)}, u32[]{:S(2)}, u32[]{:S(2)}) collective-permute-start(f32[128,1024]{1,0:T(8,128)S(1)} %copy-done.10), channel_id=1, source_target_pairs={{0,1},{1,0},{2,3},{3,2},{4,5},{5,4},{6,7},{7,6},{8,9},{9,8},{10,11... | collective-permute-start | bytes 1572872 | tf_op jit(solution)/shard_map/ppermute | solution.py:62
  218.8 13.9 %collective-permute-start.49 = (bf16[528,512]{1,0:T(8,128)(2,1)S(1)}, bf16[528,512]{1,0:T(8,128)(2,1)S(1)}, u32[]{:S(2)}, u32[]{:S(2)}) collective-permute-start(bf16[528,512]{1,0:T(8,128)(2,1)S(1)} %shard_map.302.refs_0_), channel_id=1, source_target_pairs={{0,8},{1,25},{2,10},{3,27},{4,12},{5,29},{6,14},{7,31},{8,0},{9,17... | collective-permute-start | bytes 1622024 | tf_op jit(solution)/shard_map/ppermute | solution.py:62
  220.5 19.6 %collective-permute-start.44 = (bf16[512,1024]{1,0:T(8,128)(2,1)S(1)}, bf16[512,1024]{1,0:T(8,128)(2,1)S(1)}, u32[]{:S(2)}, u32[]{:S(2)}) collective-permute-start(bf16[512,1024]{1,0:T(8,128)(2,1)S(1)} %shard_map.299.refs_0_), channel_id=1, source_target_pairs={{0,1},{1,0},{2,3},{3,2},{4,5},{5,4},{6,7},{7,6},{8,9},{9,8},{10,11... | collective-permute-start | bytes 3145736 | tf_op jit(solution)/shard_map/ppermute | solution.py:62
  220.9 19.8 %collective-permute-start.46 = (bf16[512,1024]{1,0:T(8,128)(2,1)S(1)}, bf16[512,1024]{1,0:T(8,128)(2,1)S(1)}, u32[]{:S(2)}, u32[]{:S(2)}) collective-permute-start(bf16[512,1024]{1,0:T(8,128)(2,1)S(1)} %collective-permute-done.42.refs_2_), channel_id=1, source_target_pairs={{0,1},{1,0},{2,3},{3,2},{4,5},{5,4},{6,7},{7,6},{8,9},{9,8},{10,11... | collective-permute-start | bytes 3145736 | tf_op jit(solution)/shard_map/ppermute | solution.py:62
  226.1 14.7 %collective-permute-start.45 = (bf16[512,1024]{1,0:T(8,128)(2,1)S(1)}, bf16[512,1024]{1,0:T(8,128)(2,1)S(1)}, u32[]{:S(2)}, u32[]{:S(2)}) collective-permute-start(bf16[512,1024]{1,0:T(8,128)(2,1)S(1)} %collective-permute-done.41.refs_1_), channel_id=1, source_target_pairs={{0,1},{1,0},{2,3},{3,2},{4,5},{5,4},{6,7},{7,6},{8,9},{9,8},{10,11... | collective-permute-start | bytes 3145736 | tf_op jit(solution)/shard_map/ppermute | solution.py:62
  (61 other events, 588.2 us)

commit v2 on v1

--- a/solution.py
+++ b/solution.py
@@ -173,11 +173,11 @@
         first, fc_part = refs[9:]
         first[:256, :] = out_ref[...]
         first[256:384, :] = in_ref[...]
-        first[384:, :] = jnp.zeros((EXTRA, D), bf16)
-        for k in range(8):
-            first[384 + k // 2 : 385 + k // 2, 512 * (k % 2) : 512 * (k % 2) + 512] = refs[k][...].reshape(1, 512)
-        for k in range(2):
-            first[388 + k : 389 + k, :] = refs[8][pl.ds(1024 * k, 1024)].reshape(1, 1024)
+        rows = [
+            jnp.concatenate([refs[k + n][...].astype(f32).reshape(1, 512) for n in range(2)], 1) for k in range(0, 8, 2)
+        ]
+        rows += [refs[8][pl.ds(1024 * k, 1024)].astype(f32).reshape(1, 1024) for k in range(2)]
+        first[384:, :] = jnp.concatenate([*rows, jnp.zeros((EXTRA - 6, D), f32)], 0).astype(bf16)
         fc_part[:, :1024] = low_ref[...]
         fc_part[:, 1024:] = high_ref[...]
 

time: 254 us -> 254 us (level)
  no operation moved by 1% of the time
where the time goes in v2:
time: 254 us; the launch traced here: 253 us
  starting transfers between devices  82.6 us (33%)
  Pallas kernels  78.2 us (31%)
  waiting for transfers between devices  71.3 us (28%)
  local copies, waits for them, and re-layouts  15.4 us (6%)
  between operations  4.05 us (2%)
    ppermute x55, starting transfers between devices, swap(): return lax.ppermute(array, AXES, pairs)  82.6 us
    pallas_call x25, Pallas kernels, stepped(): pl.pallas_call(body, grid_spec=pltpu.PrefetchScalarGridSpec(num_scalar_pr...  78.2 us
    ppermute x55, waiting for transfers between devices, swap(): return lax.ppermute(array, AXES, pairs)  71.3 us
    unnamed x78, local copies, waits for them, and re-layouts  8.8 us
  transfers between devices with their start and end apart: 55, of which 19 were waited for; matrix products, arithmetic and copies ran while one was open for 3% of the time, Pallas kernels for 25%

profile of v2, /device:TPU:1, one launch (start us, length us, event | category | flops | bytes accessed | tf_op | source)
XLA Modules:
  0.0 253.2 jit_solution(8337998918989354690)
XLA Ops:
  1.9 3.3 %shard_map.280 = (bf16[400,1024]{1,0:T(8,128)(2,1)}, bf16[128,2048]{1,0:T(8,128)(2,1)}) custom-call(s32[16]{0:T(128)} %get-tuple-element.184.t, bf16[128,1024]{1,0:T(8,128)(2,1)} %in_ref.5, bf16[512,1024]{1,0:T(8,128)(2,1)} %own.4, bf16[512,4096]{1,0:T(8,128)(2,1)} %w_fc.1, bf16[512,4096]{1,0:T(8,128)(2,1)} %w_fc.1, bf16[512]{0:T(512)(128)(2,1)} %gain_ref.1, ...), custom_call_target="tpu_custom_call" | custom-call | bytes 13284000 | tf_op jit(solution)/shard_map/pallas_call | solution.py:142
  5.2 3.6 %collective-permute-start.5 = (bf16[400,1024]{1,0:T(8,128)(2,1)}, bf16[400,1024]{1,0:T(8,128)(2,1)S(1)}, u32[]{:S(2)}, u32[]{:S(2)}) collective-permute-start(bf16[400,1024]{1,0:T(8,128)(2,1)} %get-tuple-element.107.own_ref), channel_id=1, source_target_pairs={{0,64},{1,97},{2,66},{3,99},{4,68},{5,101},{6,70},{7,103},{8,72},{... | collective-permute-start | bytes 2457608 | tf_op jit(solution)/shard_map/ppermute | solution.py:62
  16.0 8.2 %collective-permute-done.4.near_fc = bf16[128,2048]{1,0:T(8,128)(2,1)S(1)} collective-permute-done((bf16[128,2048]{1,0:T(8,128)(2,1)}, bf16[128,2048]{1,0:T(8,128)(2,1)S(1)}, u32[]{:S(2)}, u32[]{:S(2)}) %collective-permute-start.4) | collective-permute-done | bytes 524320 | tf_op jit(solution)/shard_map/ppermute | solution.py:62
  25.2 5.5 %shard_map.281 = (f32[128,3072]{1,0:T(8,128)S(1)}, bf16[128,3072]{1,0:T(8,128)(2,1)S(1)}) custom-call(s32[16]{0:T(128)S(1)} %copy-done.5, bf16[400,1024]{1,0:T(8,128)(2,1)S(1)} %copy-done, bf16[400,1024]{1,0:T(8,128)(2,1)} %copy-done.13, bf16[512]{0:T(512)(128)(2,1)S(1)} %copy-done.6, bf16[512]{0:T(512)(128)(2,1)S(1)} %copy-done.7, bf16[512,3072]{1,0:T(8,128)(2,1)} %own.5), custom_call_target="tpu_custom_call" | custom-call | bytes 29520000 | tf_op jit(solution)/shard_map/pallas_call | solution.py:142
  33.5 6.0 %collective-permute-start.3 = (bf16[256,2048]{1,0:T(8,128)(2,1)S(1)}, bf16[256,2048]{1,0:T(8,128)(2,1)S(1)}, u32[]{:S(2)}, u32[]{:S(2)}) collective-permute-start(bf16[256,2048]{1,0:T(8,128)(2,1)S(1)} %pad_maximum_fusion.cot_ref.refs_0_.refs_12_), channel_id=1, source_target_pairs={{0,10},{1,31},{2,8},{3,29},{4,14},{5,27},{6,12},{7,25},{8,2},{9,23... | collective-permute-start | bytes 3145736 | tf_op jit(solution)/shard_map/ppermute | solution.py:62
  39.5 3.6 %collective-permute-done.8.theirs_ref = bf16[128,3072]{1,0:T(8,128)(2,1)S(1)} collective-permute-done((bf16[128,3072]{1,0:T(8,128)(2,1)S(1)}, bf16[128,3072]{1,0:T(8,128)(2,1)S(1)}, u32[]{:S(2)}, u32[]{:S(2)}) %collective-permute-start.8) | collective-permute-done | bytes 786464 | tf_op jit(solution)/shard_map/ppermute | solution.py:62
  45.7 3.8 %collective-permute-start.6 = (bf16[128,2048]{1,0:T(8,128)(2,1)S(1)}, bf16[128,2048]{1,0:T(8,128)(2,1)S(1)}, u32[]{:S(2)}, u32[]{:S(2)}) collective-permute-start(bf16[128,2048]{1,0:T(8,128)(2,1)S(1)} %collective-permute-done.4.near_fc), channel_id=1, source_target_pairs={{0,2},{1,7},{2,0},{3,5},{4,6},{5,3},{6,4},{7,1},{8,10},{9,15},{10,... | collective-permute-start | bytes 1572872 | tf_op jit(solution)/shard_map/ppermute | solution.py:62
  52.0 5.2 %collective-permute-done.6.z_fc = bf16[128,2048]{1,0:T(8,128)(2,1)S(1)} collective-permute-done((bf16[128,2048]{1,0:T(8,128)(2,1)S(1)}, bf16[128,2048]{1,0:T(8,128)(2,1)S(1)}, u32[]{:S(2)}, u32[]{:S(2)}) %collective-permute-start.6) | collective-permute-done | bytes 524320 | tf_op jit(solution)/shard_map/ppermute | solution.py:62
  63.7 3.2 %shard_map.283 = (bf16[128,3072]{1,0:T(8,128)(2,1)S(1)}, bf16[128,1024]{1,0:T(8,128)(2,1)S(1)}) custom-call(s32[16]{0:T(128)S(1)} %copy-done.5, f32[128,3072]{1,0:T(8,128)S(1)} %get-tuple-element.112.mine_ref, bf16[128,3072]{1,0:T(8,128)(2,1)} %copy-done.37, f32[8,1024]{1,0:T(8,128)S(1)} %get-tuple-element.120.full_ref.refs_4_, s32[1,128]{1,0:T(1,128)S(1)} %copy-done.8), custom_call_target="tpu_custom_call" | custom-call | bytes 29889000 | tf_op jit(solution)/shard_map/pallas_call | solution.py:142
  68.5 7.1 %collective-permute-done.7.x_fc = bf16[256,2048]{1,0:T(8,128)(2,1)S(1)} collective-permute-done((bf16[256,2048]{1,0:T(8,128)(2,1)S(1)}, bf16[256,2048]{1,0:T(8,128)(2,1)S(1)}, u32[]{:S(2)}, u32[]{:S(2)}) %collective-permute-start.7) | collective-permute-done | bytes 1048608 | tf_op jit(solution)/shard_map/ppermute | solution.py:62
  82.0 4.8 %collective-permute-start.16 = (bf16[256,1024]{1,0:T(8,128)(2,1)}, bf16[256,1024]{1,0:T(8,128)(2,1)}, u32[]{:S(2)}, u32[]{:S(2)}) collective-permute-start(bf16[256,1024]{1,0:T(8,128)(2,1)} %pad_maximum_fusion.1.side_ref.refs_0_), channel_id=1, source_target_pairs={{0,10},{1,31},{2,8},{3,29},{4,14},{5,27},{6,12},{7,25},{8,2},{9,23... | collective-permute-start | bytes 1572872 | tf_op jit(solution)/shard_map/ppermute | solution.py:62
  87.2 10.3 %shard_map.285 = (bf16[256,2048]{1,0:T(8,128)(2,1)S(1)}, bf16[256,2048]{1,0:T(8,128)(2,1)S(1)}, f32[1,2048]{1,0:T(1,128)S(1)}, f32[128,1024]{1,0:T(8,128)S(1)}, ...) custom-call(s32[16]{0:T(128)S(1)} %copy-done.5, ...), custom_call_target="tpu_custom_call" | custom-call | bytes 44280000 | tf_op jit(solution)/shard_map/pallas_call | solution.py:142
  107.2 3.5 %shard_map.287.refs_0_.refs_1_.refs_2_.refs_3_ = bf16[1024,1024]{1,0:T(8,128)(2,1)S(1)} custom-call(s32[16]{0:T(128)S(1)} %copy-done.5, bf16[256,2048]{1,0:T(8,128)(2,1)} %copy-done.11, bf16[256,2048]{1,0:T(8,128)(2,1)} %copy-done.20, bf16[256,2048]{1,0:T(8,128)(2,1)} %copy-done.19, bf16[256,2048]{1,0:T(8,128)(2,1)} %copy-done.18, ...), custom_call_target="tpu_custom_call" | custom-call | bytes 14760000 | tf_op jit(solution)/shard_map/pallas_call | solution.py:142
  110.8 5.9 %shard_map.288 = (f32[128,1024]{1,0:T(8,128)S(1)}, bf16[2,128,2048]{2,1,0:T(8,128)(2,1)S(1)}, f32[8,1024]{1,0:T(8,128)S(1)}) custom-call(s32[16]{0:T(128)S(1)} %copy-done.5, f32[128,1024]{1,0:T(8,128)S(1)} %copy-done.4, f32[128,1024]{1,0:T(8,128)} %collective-permute-done.21.theirs_ref, f32[128,1024]{1,0:T(8,128)S(1)} %get-tuple-element.122.res_ref, ...), custom_call_target="tpu_custom_call" | custom-call | bytes 42435000 | tf_op jit(solution)/shard_map/pallas_call | solution.py:142
  120.5 4.2 %collective-permute-start.26 = (bf16[256,1536]{1,0:T(8,128)(2,1)S(1)}, bf16[256,1536]{1,0:T(8,128)(2,1)S(1)}, u32[]{:S(2)}, u32[]{:S(2)}) collective-permute-start(bf16[256,1536]{1,0:T(8,128)(2,1)S(1)} %get-tuple-element.144), channel_id=1, source_target_pairs={{0,10},{1,31},{2,8},{3,29},{4,14},{5,27},{6,12},{7,25},{8,2},{9,23... | collective-permute-start | bytes 2359304 | tf_op jit(solution)/shard_map/ppermute | solution.py:62
  125.6 4.1 %shard_map.290 = bf16[512,1024]{1,0:T(8,128)(2,1)S(1)} custom-call(s32[16]{0:T(128)S(1)} %copy-done.5, bf16[256,1024]{1,0:T(8,128)(2,1)} %pad_maximum_fusion.1.side_ref.refs_0_, bf16[256,1024]{1,0:T(8,128)(2,1)} %collective-permute-done.14.refs_1_, bf16[256,1024]{1,0:T(8,128)(2,1)} %collective-permute-done.15.refs_2_, ...), custom_call_target="tpu_custom_call" | custom-call | bytes 15867000 | tf_op jit(solution)/shard_map/pallas_call | solution.py:142
  131.0 8.8 %shard_map.291 = (f32[128,1024]{1,0:T(8,128)}, f32[32,512]{1,0:T(8,128)S(1)}) custom-call(s32[16]{0:T(128)S(1)} %copy-done.5, bf16[2,128,2048]{2,1,0:T(8,128)(2,1)S(1)} %get-tuple-element.143.mine_ref.grad_ref, bf16[512,3072]{1,0:T(8,128)(2,1)} %own.5, bf16[256,3072]{1,0:T(8,128)(2,1)} %collective-permute-done.17.a, bf16[256,3072]{1,0:T(8,128)(2,1)} %copy-done.29, ...), custom_call_target="tpu_custom_call" | custom-call | bytes 33948000 | tf_op jit(solution)/shard_map/pallas_call | solution.py:142
  139.8 3.6 %collective-permute-done.24.refs_5_.refs_9_ = bf16[256,1536]{1,0:T(8,128)(2,1)S(1)} collective-permute-done((bf16[256,1536]{1,0:T(8,128)(2,1)S(1)}, bf16[256,1536]{1,0:T(8,128)(2,1)S(1)}, u32[]{:S(2)}, u32[]{:S(2)}) %collective-permute-start.24) | collective-permute-done | bytes 786464 | tf_op jit(solution)/shard_map/ppermute | solution.py:62
  145.2 2.9 %shard_map.292 = bf16[528,512]{1,0:T(8,128)(2,1)S(1)} custom-call(s32[16]{0:T(128)S(1)} %copy-done.5, bf16[1024,1024]{1,0:T(8,128)(2,1)S(1)} %shard_map.287.refs_0_.refs_1_.refs_2_.refs_3_, bf16[1024,1024]{1,0:T(8,128)(2,1)S(1)} %shard_map.287.refs_0_.refs_1_.refs_2_.refs_3_, bf16[1024,1024]{1,0:T(8,128)(2,1)S(1)} %shard_map.287.refs_0_.refs_1_.refs_2_.refs_3_, ...), custom_call_target="tpu_custom_call" | custom-call | bytes 12177000 | tf_op jit(solution)/shard_map/pallas_call | solution.py:142
  149.3 5.6 %shard_map.293 = (bf16[128,1024]{1,0:T(8,128)(2,1)S(1)}, bf16[128,1024]{1,0:T(8,128)(2,1)S(1)}, bf16[128,1024]{1,0:T(8,128)(2,1)S(1)}, f32[128,1024]{1,0:T(8,128)S(1)}) custom-call(s32[16]{0:T(128)S(1)} %copy-done.5, bf16[256,1024]{1,0:T(8,128)(2,1)} %pad_maximum_fusion.1.side_ref.refs_0_, bf16[256,1024]{1,0:T(8,128)(2,1)} %collective-permute-done.14.refs_1_, ...), custom_call_target="tpu_custom_call" | custom-call | bytes 18450000 | tf_op jit(solution)/shard_map/pallas_call | solution.py:142
  158.5 3.6 %shard_map.294 = (bf16[272,512]{1,0:T(8,128)(2,1)S(1)}, f32[256,512]{1,0:T(8,128)S(1)}, f32[16,512]{1,0:T(8,128)S(1)}) custom-call(s32[16]{0:T(128)S(1)} %copy-done.5, bf16[1024,1024]{1,0:T(8,128)(2,1)S(1)} %shard_map.287.refs_0_.refs_1_.refs_2_.refs_3_, bf16[1024,1024]{1,0:T(8,128)(2,1)S(1)} %shard_map.287.refs_0_.refs_1_.refs_2_.refs_3_, ...), custom_call_target="tpu_custom_call" | custom-call | bytes 14391000 | tf_op jit(solution)/shard_map/pallas_call | solution.py:142
  168.4 3.9 %collective-permute-done.33.refs_0_ = bf16[128,1024]{1,0:T(8,128)(2,1)S(1)} collective-permute-done((bf16[128,1024]{1,0:T(8,128)(2,1)S(1)}, bf16[128,1024]{1,0:T(8,128)(2,1)S(1)}, u32[]{:S(2)}, u32[]{:S(2)}) %collective-permute-start.33) | collective-permute-done | bytes 262176 | tf_op jit(solution)/shard_map/ppermute | solution.py:62
  176.2 6.8 %collective-permute-done.34.received_ref = bf16[144,512]{1,0:T(8,128)(2,1)S(1)} collective-permute-done((bf16[144,512]{1,0:T(8,128)(2,1)S(1)}, bf16[144,512]{1,0:T(8,128)(2,1)S(1)}, u32[]{:S(2)}, u32[]{:S(2)}) %collective-permute-start.34) | collective-permute-done | bytes 147488 | tf_op jit(solution)/shard_map/ppermute | solution.py:62
  187.9 3.6 %collective-permute-done.38.received_ref = bf16[144,512]{1,0:T(8,128)(2,1)S(1)} collective-permute-done((bf16[144,512]{1,0:T(8,128)(2,1)S(1)}, bf16[144,512]{1,0:T(8,128)(2,1)S(1)}, u32[]{:S(2)}, u32[]{:S(2)}) %collective-permute-start.38) | collective-permute-done | bytes 147488 | tf_op jit(solution)/shard_map/ppermute | solution.py:62
  192.2 3.7 %collective-permute-done.39.other_ref = bf16[128,512]{1,0:T(8,128)(2,1)S(1)} collective-permute-done((bf16[128,512]{1,0:T(8,128)(2,1)S(1)}, bf16[128,512]{1,0:T(8,128)(2,1)S(1)}, u32[]{:S(2)}, u32[]{:S(2)}) %collective-permute-start.39) | collective-permute-done | bytes 131104 | tf_op jit(solution)/shard_map/ppermute | solution.py:62
  208.3 10.5 %collective-permute-start.13 = (f32[128,1024]{1,0:T(8,128)S(1)}, f32[128,1024]{1,0:T(8,128)S(1)}, u32[]{:S(2)}, u32[]{:S(2)}) collective-permute-start(f32[128,1024]{1,0:T(8,128)S(1)} %copy-done.10), channel_id=1, source_target_pairs={{0,1},{1,0},{2,3},{3,2},{4,5},{5,4},{6,7},{7,6},{8,9},{9,8},{10,11... | collective-permute-start | bytes 1572872 | tf_op jit(solution)/shard_map/ppermute | solution.py:62
  221.1 5.0 %collective-permute-done.50.refs_3_ = bf16[528,512]{1,0:T(8,128)(2,1)S(1)} collective-permute-done((bf16[528,512]{1,0:T(8,128)(2,1)S(1)}, bf16[528,512]{1,0:T(8,128)(2,1)S(1)}, u32[]{:S(2)}, u32[]{:S(2)}) %collective-permute-start.50) | collective-permute-done | bytes 540704 | tf_op jit(solution)/shard_map/ppermute | solution.py:62
  226.1 4.7 %collective-permute-start.45 = (bf16[512,1024]{1,0:T(8,128)(2,1)S(1)}, bf16[512,1024]{1,0:T(8,128)(2,1)S(1)}, u32[]{:S(2)}, u32[]{:S(2)}) collective-permute-start(bf16[512,1024]{1,0:T(8,128)(2,1)S(1)} %collective-permute-done.41.refs_1_), channel_id=1, source_target_pairs={{0,1},{1,0},{2,3},{3,2},{4,5},{5,4},{6,7},{7,6},{8,9},{9,8},{10,11... | collective-permute-start | bytes 3145736 | tf_op jit(solution)/shard_map/ppermute | solution.py:62
  232.8 3.2 %collective-permute-start.47 = (bf16[512,1024]{1,0:T(8,128)(2,1)S(1)}, bf16[512,1024]{1,0:T(8,128)(2,1)S(1)}, u32[]{:S(2)}, u32[]{:S(2)}) collective-permute-start(bf16[512,1024]{1,0:T(8,128)(2,1)S(1)} %collective-permute-done.43.refs_3_), channel_id=1, source_target_pairs={{0,1},{1,0},{2,3},{3,2},{4,5},{5,4},{6,7},{7,6},{8,9},{9,8},{10,11... | collective-permute-start | bytes 3145736 | tf_op jit(solution)/shard_map/ppermute | solution.py:62
  236.0 4.2 %collective-permute-done.48.refs_1_ = bf16[528,512]{1,0:T(8,128)(2,1)S(1)} collective-permute-done((bf16[528,512]{1,0:T(8,128)(2,1)S(1)}, bf16[528,512]{1,0:T(8,128)(2,1)S(1)}, u32[]{:S(2)}, u32[]{:S(2)}) %collective-permute-start.48) | collective-permute-done | bytes 540704 | tf_op jit(solution)/shard_map/ppermute | solution.py:62
  242.0 6.7 %shard_map.303 = (f32[512,4096]{1,0:T(8,128)}, f32[8,256,1024]{2,1,0:T(8,128)}) custom-call(s32[16]{0:T(128)S(1)} %copy-done.5, bf16[512,1024]{1,0:T(8,128)(2,1)S(1)} %shard_map.299.refs_0_, bf16[512,1024]{1,0:T(8,128)(2,1)S(1)} %collective-permute-done.41.refs_1_, bf16[512,1024]{1,0:T(8,128)(2,1)S(1)} %collective-permute-done.42.refs_2_, ...), custom_call_target="tpu_custom_call" | custom-call | bytes 25830000 | tf_op jit(solution)/shard_map/pallas_call | solution.py:142
  248.8 4.2 %shard_map.304 = (f32[512,3072]{1,0:T(8,128)}, f32[512,1024]{1,0:T(8,128)}, f32[512]{0:T(512)}, f32[512]{0:T(512)}, f32[512]{0:T(512)}, /*index=5*/f32[512]{0:T(...) custom-call(s32[16]{0:T(128)S(1)} %copy-done.5, ...), custom_call_target="tpu_custom_call" | custom-call | bytes 22140000 | tf_op jit(solution)/shard_map/pallas_call | solution.py:142
  (195 shorter events, 85.8 us)
Async XLA Ops:
  5.2 19.1 %collective-permute-start.5 = (bf16[400,1024]{1,0:T(8,128)(2,1)}, bf16[400,1024]{1,0:T(8,128)(2,1)S(1)}, u32[]{:S(2)}, u32[]{:S(2)}) collective-permute-start(bf16[400,1024]{1,0:T(8,128)(2,1)} %get-tuple-element.107.own_ref), channel_id=1, source_target_pairs={{0,64},{1,97},{2,66},{3,99},{4,68},{5,101},{6,70},{7,103},{8,72},{... | collective-permute-start | bytes 2457608 | tf_op jit(solution)/shard_map/ppermute | solution.py:62
  8.9 15.4 %collective-permute-start.4 = (bf16[128,2048]{1,0:T(8,128)(2,1)}, bf16[128,2048]{1,0:T(8,128)(2,1)S(1)}, u32[]{:S(2)}, u32[]{:S(2)}) collective-permute-start(bf16[128,2048]{1,0:T(8,128)(2,1)} %get-tuple-element.108), channel_id=1, source_target_pairs={{0,64},{1,97},{2,66},{3,99},{4,68},{5,101},{6,70},{7,103},{8,72},{... | collective-permute-start | bytes 1572872 | tf_op jit(solution)/shard_map/ppermute | solution.py:62
  30.8 12.3 %collective-permute-start.8 = (bf16[128,3072]{1,0:T(8,128)(2,1)S(1)}, bf16[128,3072]{1,0:T(8,128)(2,1)S(1)}, u32[]{:S(2)}, u32[]{:S(2)}) collective-permute-start(bf16[128,3072]{1,0:T(8,128)(2,1)S(1)} %get-tuple-element.114), channel_id=1, source_target_pairs={{0,64},{1,97},{2,66},{3,99},{4,68},{5,101},{6,70},{7,103},{8,72},{... | collective-permute-start | bytes 2359304 | tf_op jit(solution)/shard_map/ppermute | solution.py:62
  33.5 25.8 %collective-permute-start.3 = (bf16[256,2048]{1,0:T(8,128)(2,1)S(1)}, bf16[256,2048]{1,0:T(8,128)(2,1)S(1)}, u32[]{:S(2)}, u32[]{:S(2)}) collective-permute-start(bf16[256,2048]{1,0:T(8,128)(2,1)S(1)} %pad_maximum_fusion.cot_ref.refs_0_.refs_12_), channel_id=1, source_target_pairs={{0,10},{1,31},{2,8},{3,29},{4,14},{5,27},{6,12},{7,25},{8,2},{9,23... | collective-permute-start | bytes 3145736 | tf_op jit(solution)/shard_map/ppermute | solution.py:62
  43.0 16.4 %collective-permute-start.9 = (bf16[512,1024]{1,0:T(8,128)(2,1)S(1)}, bf16[512,1024]{1,0:T(8,128)(2,1)S(1)}, u32[]{:S(2)}, u32[]{:S(2)}) collective-permute-start(bf16[512,1024]{1,0:T(8,128)(2,1)S(1)} %get-tuple-element.115), channel_id=1, source_target_pairs={{0,64},{1,97},{2,66},{3,99},{4,68},{5,101},{6,70},{7,103},{8,72},{... | collective-permute-start | bytes 3145736 | tf_op jit(solution)/shard_map/ppermute | solution.py:62
  45.7 11.6 %collective-permute-start.6 = (bf16[128,2048]{1,0:T(8,128)(2,1)S(1)}, bf16[128,2048]{1,0:T(8,128)(2,1)S(1)}, u32[]{:S(2)}, u32[]{:S(2)}) collective-permute-start(bf16[128,2048]{1,0:T(8,128)(2,1)S(1)} %collective-permute-done.4.near_fc), channel_id=1, source_target_pairs={{0,2},{1,7},{2,0},{3,5},{4,6},{5,3},{6,4},{7,1},{8,10},{9,15},{10,... | collective-permute-start | bytes 1572872 | tf_op jit(solution)/shard_map/ppermute | solution.py:62
  49.5 19.0 %collective-permute-start.2 = (bf16[256,2048]{1,0:T(8,128)(2,1)S(1)}, bf16[256,2048]{1,0:T(8,128)(2,1)S(1)}, u32[]{:S(2)}, u32[]{:S(2)}) collective-permute-start(bf16[256,2048]{1,0:T(8,128)(2,1)S(1)} %pad_maximum_fusion.cot_ref.refs_0_.refs_12_), channel_id=1, source_target_pairs={{0,2},{1,7},{2,0},{3,5},{4,6},{5,3},{6,4},{7,1},{8,10},{9,15},{10,... | collective-permute-start | bytes 3145736 | tf_op jit(solution)/shard_map/ppermute | solution.py:62
  49.5 19.0 %collective-permute-start.1 = (bf16[256,2048]{1,0:T(8,128)(2,1)S(1)}, bf16[256,2048]{1,0:T(8,128)(2,1)S(1)}, u32[]{:S(2)}, u32[]{:S(2)}) collective-permute-start(bf16[256,2048]{1,0:T(8,128)(2,1)S(1)} %pad_maximum_fusion.cot_ref.refs_0_.refs_12_), channel_id=1, source_target_pairs={{0,8},{1,25},{2,10},{3,27},{4,12},{5,29},{6,14},{7,31},{8,0},{9,17... | collective-permute-start | bytes 3145736 | tf_op jit(solution)/shard_map/ppermute | solution.py:62
  57.3 18.3 %collective-permute-start.7 = (bf16[256,2048]{1,0:T(8,128)(2,1)S(1)}, bf16[256,2048]{1,0:T(8,128)(2,1)S(1)}, u32[]{:S(2)}, u32[]{:S(2)}) collective-permute-start(bf16[256,2048]{1,0:T(8,128)(2,1)S(1)} %constant_dynamic-update-slice_fusion.2), channel_id=1, source_target_pairs={{0,8},{1,25},{2,10},{3,27},{4,12},{5,29},{6,14},{7,31},{8,0},{9,17... | collective-permute-start | bytes 3145736 | tf_op jit(solution)/shard_map/ppermute | solution.py:62
  59.5 19.1 %collective-permute-start.11 = (bf16[512,1024]{1,0:T(8,128)(2,1)S(1)}, bf16[512,1024]{1,0:T(8,128)(2,1)S(1)}, u32[]{:S(2)}, u32[]{:S(2)}) collective-permute-start(bf16[512,1024]{1,0:T(8,128)(2,1)S(1)} %get-tuple-element.124), channel_id=1, source_target_pairs={{0,64},{1,97},{2,66},{3,99},{4,68},{5,101},{6,70},{7,103},{8,72},{... | collective-permute-start | bytes 3145736 | tf_op jit(solution)/shard_map/ppermute | solution.py:62
  61.8 39.4 %collective-permute-start.17 = (bf16[256,3072]{1,0:T(8,128)(2,1)}, bf16[256,3072]{1,0:T(8,128)(2,1)}, u32[]{:S(2)}, u32[]{:S(2)}) collective-permute-start(bf16[256,3072]{1,0:T(8,128)(2,1)} %constant_dynamic-slice_fusion), channel_id=1, source_target_pairs={{0,64},{1,97},{2,66},{3,99},{4,68},{5,101},{6,70},{7,103},{8,72},{... | collective-permute-start | bytes 4718600 | tf_op jit(solution)/shard_map/ppermute | solution.py:62
  82.0 19.2 %collective-permute-start.16 = (bf16[256,1024]{1,0:T(8,128)(2,1)}, bf16[256,1024]{1,0:T(8,128)(2,1)}, u32[]{:S(2)}, u32[]{:S(2)}) collective-permute-start(bf16[256,1024]{1,0:T(8,128)(2,1)} %pad_maximum_fusion.1.side_ref.refs_0_), channel_id=1, source_target_pairs={{0,10},{1,31},{2,8},{3,29},{4,14},{5,27},{6,12},{7,25},{8,2},{9,23... | collective-permute-start | bytes 1572872 | tf_op jit(solution)/shard_map/ppermute | solution.py:62
  86.9 14.3 %collective-permute-start.15 = (bf16[256,1024]{1,0:T(8,128)(2,1)}, bf16[256,1024]{1,0:T(8,128)(2,1)}, u32[]{:S(2)}, u32[]{:S(2)}) collective-permute-start(bf16[256,1024]{1,0:T(8,128)(2,1)} %pad_maximum_fusion.1.side_ref.refs_0_), channel_id=1, source_target_pairs={{0,2},{1,7},{2,0},{3,5},{4,6},{5,3},{6,4},{7,1},{8,10},{9,15},{10,... | collective-permute-start | bytes 1572872 | tf_op jit(solution)/shard_map/ppermute | solution.py:62
  86.9 14.3 %collective-permute-start.14 = (bf16[256,1024]{1,0:T(8,128)(2,1)}, bf16[256,1024]{1,0:T(8,128)(2,1)}, u32[]{:S(2)}, u32[]{:S(2)}) collective-permute-start(bf16[256,1024]{1,0:T(8,128)(2,1)} %pad_maximum_fusion.1.side_ref.refs_0_), channel_id=1, source_target_pairs={{0,8},{1,25},{2,10},{3,27},{4,12},{5,29},{6,14},{7,31},{8,0},{9,17... | collective-permute-start | bytes 1572872 | tf_op jit(solution)/shard_map/ppermute | solution.py:62
  99.9 10.8 %collective-permute-start.21 = (f32[128,1024]{1,0:T(8,128)}, f32[128,1024]{1,0:T(8,128)}, u32[]{:S(2)}, u32[]{:S(2)}) collective-permute-start(f32[128,1024]{1,0:T(8,128)} %get-tuple-element.141), channel_id=1, source_target_pairs={{0,1},{1,0},{2,3},{3,2},{4,5},{5,4},{6,7},{7,6},{8,9},{9,8},{10,11... | collective-permute-start | bytes 1572872 | tf_op jit(solution)/shard_map/ppermute | solution.py:62
  102.0 14.8 %collective-permute-start.18 = (bf16[256,1024]{1,0:T(8,128)(2,1)S(1)}, bf16[256,1024]{1,0:T(8,128)(2,1)S(1)}, u32[]{:S(2)}, u32[]{:S(2)}) collective-permute-start(bf16[256,1024]{1,0:T(8,128)(2,1)S(1)} %get-tuple-element.134), channel_id=1, source_target_pairs={{0,8},{1,25},{2,10},{3,27},{4,12},{5,29},{6,14},{7,31},{8,0},{9,17... | collective-permute-start | bytes 1572872 | tf_op jit(solution)/shard_map/ppermute | solution.py:62
  104.5 14.9 %collective-permute-start.19 = (bf16[256,1024]{1,0:T(8,128)(2,1)S(1)}, bf16[256,1024]{1,0:T(8,128)(2,1)S(1)}, u32[]{:S(2)}, u32[]{:S(2)}) collective-permute-start(bf16[256,1024]{1,0:T(8,128)(2,1)S(1)} %get-tuple-element.135), channel_id=1, source_target_pairs={{0,2},{1,7},{2,0},{3,5},{4,6},{5,3},{6,4},{7,1},{8,10},{9,15},{10,... | collective-permute-start | bytes 1572872 | tf_op jit(solution)/shard_map/ppermute | solution.py:62
  107.2 12.2 %collective-permute-start.20 = (bf16[256,1024]{1,0:T(8,128)(2,1)S(1)}, bf16[256,1024]{1,0:T(8,128)(2,1)S(1)}, u32[]{:S(2)}, u32[]{:S(2)}) collective-permute-start(bf16[256,1024]{1,0:T(8,128)(2,1)S(1)} %get-tuple-element.136), channel_id=1, source_target_pairs={{0,10},{1,31},{2,8},{3,29},{4,14},{5,27},{6,12},{7,25},{8,2},{9,23... | collective-permute-start | bytes 1572872 | tf_op jit(solution)/shard_map/ppermute | solution.py:62
  120.5 19.4 %collective-permute-start.26 = (bf16[256,1536]{1,0:T(8,128)(2,1)S(1)}, bf16[256,1536]{1,0:T(8,128)(2,1)S(1)}, u32[]{:S(2)}, u32[]{:S(2)}) collective-permute-start(bf16[256,1536]{1,0:T(8,128)(2,1)S(1)} %get-tuple-element.144), channel_id=1, source_target_pairs={{0,10},{1,31},{2,8},{3,29},{4,14},{5,27},{6,12},{7,25},{8,2},{9,23... | collective-permute-start | bytes 2359304 | tf_op jit(solution)/shard_map/ppermute | solution.py:62
  124.7 18.8 %collective-permute-start.24 = (bf16[256,1536]{1,0:T(8,128)(2,1)S(1)}, bf16[256,1536]{1,0:T(8,128)(2,1)S(1)}, u32[]{:S(2)}, u32[]{:S(2)}) collective-permute-start(bf16[256,1536]{1,0:T(8,128)(2,1)S(1)} %get-tuple-element.145), channel_id=1, source_target_pairs={{0,8},{1,25},{2,10},{3,27},{4,12},{5,29},{6,14},{7,31},{8,0},{9,17... | collective-permute-start | bytes 2359304 | tf_op jit(solution)/shard_map/ppermute | solution.py:62
  125.6 17.8 %collective-permute-start.25 = (bf16[256,1536]{1,0:T(8,128)(2,1)S(1)}, bf16[256,1536]{1,0:T(8,128)(2,1)S(1)}, u32[]{:S(2)}, u32[]{:S(2)}) collective-permute-start(bf16[256,1536]{1,0:T(8,128)(2,1)S(1)} %get-tuple-element.146), channel_id=1, source_target_pairs={{0,2},{1,7},{2,0},{3,5},{4,6},{5,3},{6,4},{7,1},{8,10},{9,15},{10,... | collective-permute-start | bytes 2359304 | tf_op jit(solution)/shard_map/ppermute | solution.py:62
  129.7 18.6 %collective-permute-start.27 = (bf16[512,1024]{1,0:T(8,128)(2,1)S(1)}, bf16[512,1024]{1,0:T(8,128)(2,1)S(1)}, u32[]{:S(2)}, u32[]{:S(2)}) collective-permute-start(bf16[512,1024]{1,0:T(8,128)(2,1)S(1)} %shard_map.290), channel_id=1, source_target_pairs={{0,64},{1,97},{2,66},{3,99},{4,68},{5,101},{6,70},{7,103},{8,72},{... | collective-permute-start | bytes 3145736 | tf_op jit(solution)/shard_map/ppermute | solution.py:62
  173.0 10.6 %collective-permute-start.37 = (bf16[128,1024]{1,0:T(8,128)(2,1)S(1)}, bf16[128,1024]{1,0:T(8,128)(2,1)S(1)}, u32[]{:S(2)}, u32[]{:S(2)}) collective-permute-start(bf16[128,1024]{1,0:T(8,128)(2,1)S(1)} %shard_map.297.refs_3_), channel_id=1, source_target_pairs={{0,6},{1,3},{2,4},{3,1},{4,2},{5,7},{6,0},{7,5},{8,14},{9,11},{10,... | collective-permute-start | bytes 786440 | tf_op jit(solution)/shard_map/ppermute | solution.py:62
  184.2 17.3 %collective-permute-start.41 = (bf16[512,1024]{1,0:T(8,128)(2,1)S(1)}, bf16[512,1024]{1,0:T(8,128)(2,1)S(1)}, u32[]{:S(2)}, u32[]{:S(2)}) collective-permute-start(bf16[512,1024]{1,0:T(8,128)(2,1)S(1)} %shard_map.299.refs_0_), channel_id=1, source_target_pairs={{0,2},{1,7},{2,0},{3,5},{4,6},{5,3},{6,4},{7,1},{8,10},{9,15},{10,... | collective-permute-start | bytes 3145736 | tf_op jit(solution)/shard_map/ppermute | solution.py:62
  186.1 34.4 %collective-permute-start.42 = (bf16[512,1024]{1,0:T(8,128)(2,1)S(1)}, bf16[512,1024]{1,0:T(8,128)(2,1)S(1)}, u32[]{:S(2)}, u32[]{:S(2)}) collective-permute-start(bf16[512,1024]{1,0:T(8,128)(2,1)S(1)} %shard_map.299.refs_0_), channel_id=1, source_target_pairs={{0,8},{1,25},{2,10},{3,27},{4,12},{5,29},{6,14},{7,31},{8,0},{9,17... | collective-permute-start | bytes 3145736 | tf_op jit(solution)/shard_map/ppermute | solution.py:62
  201.5 29.3 %collective-permute-start.43 = (bf16[512,1024]{1,0:T(8,128)(2,1)S(1)}, bf16[512,1024]{1,0:T(8,128)(2,1)S(1)}, u32[]{:S(2)}, u32[]{:S(2)}) collective-permute-start(bf16[512,1024]{1,0:T(8,128)(2,1)S(1)} %collective-permute-done.41.refs_1_), channel_id=1, source_target_pairs={{0,8},{1,25},{2,10},{3,27},{4,12},{5,29},{6,14},{7,31},{8,0},{9,17... | collective-permute-start | bytes 3145736 | tf_op jit(solution)/shard_map/ppermute | solution.py:62
  206.1 20.0 %collective-permute-start.50 = (bf16[528,512]{1,0:T(8,128)(2,1)S(1)}, bf16[528,512]{1,0:T(8,128)(2,1)S(1)}, u32[]{:S(2)}, u32[]{:S(2)}) collective-permute-start(bf16[528,512]{1,0:T(8,128)(2,1)S(1)} %shard_map.302.refs_0_), channel_id=1, source_target_pairs={{0,10},{1,31},{2,8},{3,29},{4,14},{5,27},{6,12},{7,25},{8,2},{9,23... | collective-permute-start | bytes 1622024 | tf_op jit(solution)/shard_map/ppermute | solution.py:62
  208.3 12.6 %collective-permute-start.13 = (f32[128,1024]{1,0:T(8,128)S(1)}, f32[128,1024]{1,0:T(8,128)S(1)}, u32[]{:S(2)}, u32[]{:S(2)}) collective-permute-start(f32[128,1024]{1,0:T(8,128)S(1)} %copy-done.10), channel_id=1, source_target_pairs={{0,1},{1,0},{2,3},{3,2},{4,5},{5,4},{6,7},{7,6},{8,9},{9,8},{10,11... | collective-permute-start | bytes 1572872 | tf_op jit(solution)/shard_map/ppermute | solution.py:62
  218.8 13.9 %collective-permute-start.49 = (bf16[528,512]{1,0:T(8,128)(2,1)S(1)}, bf16[528,512]{1,0:T(8,128)(2,1)S(1)}, u32[]{:S(2)}, u32[]{:S(2)}) collective-permute-start(bf16[528,512]{1,0:T(8,128)(2,1)S(1)} %shard_map.302.refs_0_), channel_id=1, source_target_pairs={{0,8},{1,25},{2,10},{3,27},{4,12},{5,29},{6,14},{7,31},{8,0},{9,17... | collective-permute-start | bytes 1622024 | tf_op jit(solution)/shard_map/ppermute | solution.py:62
  220.5 19.6 %collective-permute-start.44 = (bf16[512,1024]{1,0:T(8,128)(2,1)S(1)}, bf16[512,1024]{1,0:T(8,128)(2,1)S(1)}, u32[]{:S(2)}, u32[]{:S(2)}) collective-permute-start(bf16[512,1024]{1,0:T(8,128)(2,1)S(1)} %shard_map.299.refs_0_), channel_id=1, source_target_pairs={{0,1},{1,0},{2,3},{3,2},{4,5},{5,4},{6,7},{7,6},{8,9},{9,8},{10,11... | collective-permute-start | bytes 3145736 | tf_op jit(solution)/shard_map/ppermute | solution.py:62
  220.9 19.8 %collective-permute-start.46 = (bf16[512,1024]{1,0:T(8,128)(2,1)S(1)}, bf16[512,1024]{1,0:T(8,128)(2,1)S(1)}, u32[]{:S(2)}, u32[]{:S(2)}) collective-permute-start(bf16[512,1024]{1,0:T(8,128)(2,1)S(1)} %collective-permute-done.42.refs_2_), channel_id=1, source_target_pairs={{0,1},{1,0},{2,3},{3,2},{4,5},{5,4},{6,7},{7,6},{8,9},{9,8},{10,11... | collective-permute-start | bytes 3145736 | tf_op jit(solution)/shard_map/ppermute | solution.py:62
  226.1 14.7 %collective-permute-start.45 = (bf16[512,1024]{1,0:T(8,128)(2,1)S(1)}, bf16[512,1024]{1,0:T(8,128)(2,1)S(1)}, u32[]{:S(2)}, u32[]{:S(2)}) collective-permute-start(bf16[512,1024]{1,0:T(8,128)(2,1)S(1)} %collective-permute-done.41.refs_1_), channel_id=1, source_target_pairs={{0,1},{1,0},{2,3},{3,2},{4,5},{5,4},{6,7},{7,6},{8,9},{9,8},{10,11... | collective-permute-start | bytes 3145736 | tf_op jit(solution)/shard_map/ppermute | solution.py:62
  (61 other events, 588.2 us)
